TPU v7x, 512 devices: a whole 4x8x8 slice. The times are simulated.
512 devices in a mesh: dp: 4 (over x), fsdp: 128 (over y, z, core).
Axes of the slice: x: 4, y: 8, z: 8, core: 2. Of those that a mesh axis runs over, the one named last changes fastest.
Arguments:
- frames: bfloat16 [65536, 1280], P(('dp', 'fsdp')), may hold values from -6 to 6
- live_frame_count: int32 [512], P(('dp', 'fsdp')), may hold values from 1 to 128, 49152 in all
- encoder_norm_gain: bfloat16 [1280], replicated, may hold values from 0.099609375 to 1.8984375
- encoder_quantized: bfloat16 [1280, 1280], P('fsdp'), may hold values from -0.15625 to 0.15625
- encoder_block_scale: bfloat16 [1280, 20], P('fsdp'), may hold values from 0.5 to 2
- text_token_embedding: bfloat16 [49152, 5120], P(('dp', 'fsdp')), may hold values from -6 to 6
- live_text_count: int32 [512], P(('dp', 'fsdp')), may hold values from 1 to 96, 36864 in all
- decoder_norm_gain: bfloat16 [5120], replicated, may hold values from 0.099609375 to 1.8984375
- value_quantized: bfloat16 [5120, 1024], P('fsdp'), may hold values from -0.078125 to 0.078125
- value_block_scale: bfloat16 [5120, 16], P('fsdp'), may hold values from 0.5 to 2
- adapter_down_factor: bfloat16 [5120, 64], P('fsdp'), may hold values from -0.078125 to 0.078125
- adapter_up_factor: bfloat16 [1024, 64], replicated, may hold values from -0.375 to 0.375
- audio_value_gradient: bfloat16 [16384, 1024], P(('dp', 'fsdp')), may hold values from -6 to 6
- text_value_gradient: bfloat16 [49152, 1024], P(('dp', 'fsdp')), may hold values from -24 to 24
Outputs:
- audio_values: bfloat16 [16384, 1024], P(('dp', 'fsdp'))
- text_values: bfloat16 [49152, 1024], P(('dp', 'fsdp'))
- audio_grad: bfloat16 [16384, 5120], P(('dp', 'fsdp'))
- text_grad: bfloat16 [49152, 5120], P(('dp', 'fsdp'))
- grad_down: float32 [5120, 64], P('fsdp')
- up_factor_gradient: float32 [1024, 64], P('fsdp')
All inputs are finite; a program needn't handle non-finite values. No bound on the sum of `live_frame_count` or of `live_text_count` on one device may be relied on, other than what follows from the above.
Results may differ from a plain program's by a relative error of at most 0.007.
Values may be sent and summed in bfloat16 or wider, within the bound.
A program may use at most 192 MiB of HBM per device.

v0:
```python
import math

import jax
import jax.numpy as jnp
from jax import lax
from jax.sharding import PartitionSpec as P

BLOCK = 64


adapter_scale = 2.0
epsilon = 1e-05


def dequant(packed, scales):
    height, breadth = packed.shape
    blocks = (
        packed.astype(jnp.float32).reshape(height, breadth // BLOCK, BLOCK)
        * scales.astype(jnp.float32)[:, :, None]
    )
    return blocks.reshape(height, breadth).astype(jnp.bfloat16)


def contract_trailing(left, right):
    return lax.dot_general(
        left, right, (((1,), (1,)), ((), ())), preferred_element_type=jnp.float32
    )


def contract_leading(left, right):
    return lax.dot_general(
        left, right, (((0,), (0,)), ((), ())), preferred_element_type=jnp.float32
    )


def shards(
    frames,
    live_frame_count,
    encoder_norm_gain,
    encoder_quantized,
    encoder_block_scale,
    text_token_embedding,
    live_text_count,
    decoder_norm_gain,
    value_quantized,
    value_block_scale,
    adapter_down_factor,
    adapter_up_factor,
    audio_value_gradient,
    text_value_gradient,
):
    fsdp_count = lax.axis_size("fsdp")
    replica_count = lax.axis_size("dp")
    frame_rows = frames.shape[0]
    enc_width = frames.shape[1]
    signal = frames.astype(jnp.float32)
    center = signal - jnp.mean(signal, axis=1, keepdims=True)
    variance = jnp.mean(center * center, axis=1, keepdims=True)
    enc_normed = (
        center * lax.rsqrt(variance + epsilon) * encoder_norm_gain.astype(jnp.float32)
    ).astype(jnp.bfloat16)
    pieces = (
        lax.all_gather(encoder_quantized, "fsdp", axis=0, tiled=True),
        lax.all_gather(encoder_block_scale, "fsdp", axis=0, tiled=True),
    )
    weight = dequant(pieces[0], pieces[1])
    columns = enc_normed
    hidden = jnp.dot(columns, weight, preferred_element_type=jnp.float32)
    live = (jnp.arange(frame_rows) < live_frame_count[0]).astype(jnp.float32)
    encoded = ((signal + jax.nn.gelu(hidden, approximate=False)) * live[:, None]).astype(
        jnp.bfloat16
    )
    audio_rows = frame_rows // 4
    audio = encoded.reshape(audio_rows, 4 * enc_width)
    input_rows = jnp.concatenate([audio, text_token_embedding], axis=0)
    text_rows = text_token_embedding.shape[0]
    text_mask = (jnp.arange(text_rows) < live_text_count[0]).astype(jnp.bfloat16)
    output_gradient = jnp.concatenate(
        [audio_value_gradient, text_value_gradient * text_mask[:, None]], axis=0
    )
    token_rows = input_rows.shape[0]
    dec_signal = input_rows.astype(jnp.float32)
    inverse = lax.rsqrt(jnp.mean(dec_signal * dec_signal, axis=1, keepdims=True) + epsilon)
    gains = decoder_norm_gain.astype(jnp.float32)
    normalized_input = (dec_signal * inverse * gains).astype(jnp.bfloat16)
    lowrank_backward = (
        adapter_scale
        * jnp.dot(output_gradient, adapter_up_factor, preferred_element_type=jnp.float32)
    ).astype(jnp.bfloat16)
    pieces = (
        lax.all_gather(value_quantized, "fsdp", axis=0, tiled=True),
        lax.all_gather(value_block_scale, "fsdp", axis=0, tiled=True),
        lax.all_gather(adapter_down_factor, "fsdp", axis=0, tiled=True),
    )
    weight = dequant(pieces[0], pieces[1])
    columns = normalized_input
    value_acc = jnp.dot(columns, weight, preferred_element_type=jnp.float32)
    adapter_acc = jnp.dot(columns, pieces[2], preferred_element_type=jnp.float32)
    section = contract_trailing(output_gradient, weight) + contract_trailing(
        lowrank_backward, pieces[2]
    )
    value_output = value_acc
    adapter_hidden = adapter_acc.astype(jnp.bfloat16)
    value_output = value_output + adapter_scale * contract_trailing(
        adapter_hidden, adapter_up_factor
    )
    value_output = value_output.astype(jnp.bfloat16)
    weighted = section * gains
    cubed = inverse * inverse * inverse
    input_gradient = (
        inverse * weighted
        - dec_signal * cubed * jnp.mean(weighted * dec_signal, axis=1, keepdims=True)
    ).astype(jnp.bfloat16)
    gradient_multiplier = 1.0 / math.sqrt(replica_count * fsdp_count * token_rows)
    local_down = contract_leading(normalized_input, lowrank_backward) * gradient_multiplier
    device_up_factor = (
        adapter_scale * contract_leading(output_gradient, adapter_hidden) * gradient_multiplier
    )
    down_rows = local_down.shape[0] // fsdp_count
    up_rows = device_up_factor.shape[0] // fsdp_count
    summed_down, summed_up = lax.psum((local_down, device_up_factor), ("dp", "fsdp"))
    position = lax.axis_index("fsdp")
    out_down = lax.dynamic_slice_in_dim(summed_down, position * down_rows, down_rows, 0)
    out_up = lax.dynamic_slice_in_dim(summed_up, position * up_rows, up_rows, 0)
    return (
        value_output[:audio_rows],
        value_output[audio_rows:],
        input_gradient[:audio_rows],
        input_gradient[audio_rows:],
        out_down,
        out_up,
    )


def solution(mesh):
    in_specs = (
        P(("dp", "fsdp"), None),
        P(("dp", "fsdp")),
        P(),
        P("fsdp", None),
        P("fsdp", None),
        P(("dp", "fsdp"), None),
        P(("dp", "fsdp")),
        P(),
        P("fsdp", None),
        P("fsdp", None),
        P("fsdp", None),
        P(),
        P(("dp", "fsdp"), None),
        P(("dp", "fsdp"), None),
    )
    out_specs = (
        P(("dp", "fsdp"), None),
        P(("dp", "fsdp"), None),
        P(("dp", "fsdp"), None),
        P(("dp", "fsdp"), None),
        P("fsdp", None),
        P("fsdp", None),
    )
    return jax.shard_map(shards, mesh=mesh, in_specs=in_specs, out_specs=out_specs, check_vma=False)
```

profile of v0, /device:TPU:1, one launch (start us, length us, event | category | flops | bytes accessed | tf_op | source)
XLA Modules:
  0.0 516.7 jit_solution(2497891507376518578)
XLA Ops:
  7.2 0.0 copy-start
  7.2 0.0 all-gather.8.cloned.1.call-start
  7.2 0.7 all-gather.8.cloned.1.call-update
  7.9 0.0 all-gather.6.cloned.1.call-start
  8.0 0.7 all-gather.6.cloned.1.call-update
  8.7 0.0 all-reduce.3.cloned.1.call-start
  8.7 59.0 %all-gather.1 = bf16[128,10,20]{2,1,0:T(8,128)(2,1)S(1)} all-gather(bf16[1,10,20]{2,1,0:T(8,128)(2,1)} %bitcast.28), channel_id=1, replica_groups=mesh['dp'=4,'fsdp'=128] {'fsdp'}, dimensions={0}, use_global_device_ids=true | all-gather | bytes 51600 | tf_op jit(solution)/shard_map/all_gather | solution.py:64
  67.7 0.4 copy.28
  68.1 0.3 copy.29
  68.4 0.6 reshape.73
  69.0 3.2 mul.175
  72.2 8.2 %copy.30 = f32[1280,1280]{1,0:T(8,128)} copy(f32[1280,1280]{0,1:T(8,128)} %bitcast.26) | data formatting | bytes 13107200 | tf_op jit(solution)/shard_map/mul | solution.py:18
  80.4 0.0 copy-start.6
  81.8 49.1 %all-gather.2 = bf16[128,40,16]{1,2,0:T(8,128)(2,1)S(1)} all-gather(bf16[1,40,16]{1,2,0:T(8,128)(2,1)S(1)} %bitcast.29), channel_id=1, replica_groups=mesh['dp'=4,'fsdp'=128] {'fsdp'}, dimensions={0}, use_global_device_ids=true | all-gather | bytes 165120 | tf_op jit(solution)/shard_map/all_gather | solution.py:92
  130.9 0.5 copy.32
  131.4 0.0 copy-start.4
  131.4 0.2 copy.33
  131.6 0.5 reshape.74
  132.2 0.1 convert_reduce_fusion
  132.4 0.2 fusion.15
  132.6 49.9 %all_gather.19 = bf16[5120,64]{1,0:T(8,128)(2,1)S(1)} all-gather(bf16[40,64]{1,0:T(8,128)(2,1)S(1)} %copy-done.6), channel_id=1, replica_groups=mesh['dp'=4,'fsdp'=128] {'fsdp'}, dimensions={0}, use_global_device_ids=true | all-gather | bytes 660480 | tf_op jit(solution)/shard_map/all_gather | solution.py:93
  182.5 0.1 broadcast_multiply_fusion
  182.6 0.2 fusion.12
  182.8 0.0 all-gather.8.cloned.1.call-done
  182.9 7.9 %reshape.72 = f32[1280,1280]{1,0:T(8,128)} reshape(bf16[128,10,1280]{2,1,0:T(8,128)(2,1)} %all-gather.8.cloned.1.call-done) | data formatting | bytes 9830400 | tf_op jit(solution)/shard_map/convert_element_type | solution.py:18
  190.8 6.9 %fusion.19 = bf16[128,1280]{1,0:T(8,128)(2,1)S(1)} fusion(bf16[128,1280]{1,0:T(8,128)(2,1)S(1)} %copy-done.3, f32[1280,1280]{1,0:T(8,128)} %reshape.72, f32[1280,1280]{1,0:T(8,128)} %copy.30, f32[128]{0:T(128)S(1)} %compare_convert_fusion.1, f32[1280]{0:T(1024)S(1)} %convert_element_type.66, f32[128]{0:T(128)S(1)} %add_rsqrt_fusion.1, ...), kind=kOutput, calls=%fused_computation.36 | convolution fusion | flops 434667520 | bytes 13769216 | tf_op jit(solution)/shard_map/dot_general | solution.py:68
  197.7 0.2 reshape.65
  197.9 0.0 all-gather.6.cloned.1.call-done
  198.0 13.9 %copy.31 = bf16[5120,1024]{0,1:T(8,128)(2,1)} copy(bf16[5120,1024]{1,0:T(8,128)(2,1)} %all-gather.6.cloned.1.call-done) | data formatting | bytes 20971520 | tf_op jit(solution)/shard_map/all_gather | solution.py:91
  211.8 6.6 %fusion = bf16[5120,1024]{0,1:T(8,128)(2,1)S(1)} fusion(bf16[5120,1024]{0,1:T(8,128)(2,1)} %copy.31, f32[5120,16]{0,1:T(8,128)S(1)} %reshape.74), kind=kLoop, calls=%fused_computation.1 | loop fusion | flops 15728640 | bytes 21299200 | tf_op jit(solution)/shard_map/convert_element_type | solution.py:21
  218.4 0.0 copy-start.2
  218.5 1.5 fusion.33
  220.0 2.4 copy-done.1
  222.4 1.1 fusion.9
  223.5 0.7 convolution_convert_fusion
  224.3 2.1 convolution_multiply_fusion
  226.4 0.7 fusion.8
  227.1 1.0 slice.19
  228.1 0.7 slice.18
  228.9 1.1 convolution_multiply_fusion.1
  229.9 0.0 all-reduce.3.cloned.1.call-update
  229.9 7.6 %fusion.39 = f32[128,1024]{1,0:T(8,128)S(1)} fusion(bf16[5120,1024]{0,1:T(8,128)(2,1)} %copy-done.1, f32[5120]{0:T(1024)S(1)} %convert_element_type.74, f32[128]{0:T(128)S(1)} %get-tuple-element.11, bf16[96,5120]{1,0:T(8,128)(2,1)S(1)} %copy-done.2, bf16[32,5120]{1,0:T(8,128)(2,1)S(1)} %reshape.65), kind=kOutput, calls=%fused_computation.72 | convolution fusion | flops 1346764800 | bytes 12341760 | tf_op jit(solution)/shard_map/dot_general | solution.py:97
  237.5 0.2 fusion.11
  237.8 0.7 slice.17
  238.5 0.6 slice.16
  239.1 268.4 %all-reduce.3.cloned.1.call-done = (f32[5120,64]{1,0:T(8,128)}, f32[1024,64]{1,0:T(8,128)}) async-done(((f32[5120,64]{1,0:T(8,128)}, f32[1024,64]{1,0:T(8,128)}), (f32[5120,64]{1,0:T(8,128)}, f32[1024,64]{1,0:T(8,128)})) %all-reduce.3.cloned.1.call-update) | async-done | bytes 1572880 | tf_op jit(solution)/shard_map/psum | solution.py:121
  507.6 1.3 constant_dynamic-slice_fusion.1
  508.9 1.3 constant_dynamic-slice_fusion
  (22 shorter events, 0.1 us)
Async XLA Ops:
  7.2 175.4 %copy-start = (bf16[1024,64]{0,1:T(8,128)(2,1)S(1)}, bf16[1024,64]{0,1:T(8,128)(2,1)}, u32[]{:S(2)}) copy-start(bf16[1024,64]{0,1:T(8,128)(2,1)} %param.25) | copy-start | bytes 393220
  7.2 175.7 %all-gather.8.cloned.1.call-start = ((), (), s32[]{:S(2)}) async-start(), calls=%async_computation.1 | async-start | bytes 5283840 | tf_op jit(solution)/shard_map/all_gather | solution.py:63
  7.9 190.0 %all-gather.6.cloned.1.call-start = ((), (), s32[]{:S(2)}) async-start(), calls=%async_computation | async-start | bytes 10567680 | tf_op jit(solution)/shard_map/all_gather | solution.py:91
  8.7 498.9 %all-reduce.3.cloned.1.call-start = ((), (), s32[]{:S(2)}) async-start(), calls=%async_computation.2 | async-start | bytes 6291456 | tf_op jit(solution)/shard_map/psum | solution.py:121
  72.2 8.2 %copy-start.9 = (bf16[1280]{0:T(1024)(128)(2,1)S(1)}, bf16[1280]{0:T(1024)(128)(2,1)}, u32[]{:S(2)}) copy-start(bf16[1280]{0:T(1024)(128)(2,1)} %param.16) | copy-start | bytes 7684
  72.2 9.5 %copy-start.8 = (bf16[40,16]{0,1:T(8,128)(2,1)S(1)}, bf16[40,16]{0,1:T(8,128)(2,1)}, u32[]{:S(2)}) copy-start(bf16[40,16]{0,1:T(8,128)(2,1)} %param.23) | copy-start | bytes 3844
  80.4 51.8 %copy-start.7 = (bf16[5120]{0:T(1024)(128)(2,1)S(1)}, bf16[5120]{0:T(1024)(128)(2,1)}, u32[]{:S(2)}) copy-start(bf16[5120]{0:T(1024)(128)(2,1)} %param.21) | copy-start | bytes 30724
  80.4 51.8 %copy-start.3 = (bf16[128,1280]{1,0:T(8,128)(2,1)S(1)}, bf16[128,1280]{1,0:T(8,128)(2,1)}, u32[]{:S(2)}) copy-start(bf16[128,1280]{1,0:T(8,128)(2,1)} %param.14) | copy-start | bytes 983044
  80.4 52.2 %copy-start.6 = (bf16[40,64]{1,0:T(8,128)(2,1)S(1)}, bf16[40,64]{1,0:T(8,128)(2,1)}, u32[]{:S(2)}) copy-start(bf16[40,64]{1,0:T(8,128)(2,1)} %param.24) | copy-start | bytes 15364
  130.8 51.7 %copy-start.5 = (bf16[96,1024]{1,0:T(8,128)(2,1)S(1)}, bf16[96,1024]{1,0:T(8,128)(2,1)}, u32[]{:S(2)}) copy-start(bf16[96,1024]{1,0:T(8,128)(2,1)} %param.27) | copy-start | bytes 589828
  131.4 51.2 %copy-start.4 = (bf16[32,1024]{1,0:T(8,128)(2,1)S(1)}, bf16[32,1024]{1,0:T(8,128)(2,1)}, u32[]{:S(2)}) copy-start(bf16[32,1024]{1,0:T(8,128)(2,1)} %param.26) | copy-start | bytes 196612
  218.4 4.0 copy-start.1
  218.4 4.0 copy-start.2
Sparse Core Ops, SparseCore 0:
  11.1 91.5 all-gather.7
  105.9 88.8 all-gather.5
  230.1 277.4 all-reduce.2
where the time goes:
time: 518 us; the launch traced here: 517 us
  waiting for transfers between devices  270 us (52%)
  blocking collectives  158 us (31%)
  local copies, waits for them, and re-layouts  44.2 us (9%)
  matrix products  21.5 us (4%)
  between operations  15.3 us (3%)
  other arithmetic  7.79 us (2%)
    psum x1, waiting for transfers between devices, shards(): lax.psum((local_down, device_up_factor), ('dp', 'fsdp'))  268 us
    all_gather x1, blocking collectives, shards(): lax.all_gather(encoder_block_scale, 'fsdp', axis=0, tiled=True)  59 us
    all_gather x1, blocking collectives, shards(): lax.all_gather(adapter_down_factor, 'fsdp', axis=0, tiled=True)  49.9 us
    all_gather x1, blocking collectives, shards(): lax.all_gather(value_block_scale, 'fsdp', axis=0, tiled=True)  49.1 us
    all_gather x1, local copies, waits for them, and re-layouts, shards(): lax.all_gather(value_quantized, 'fsdp', axis=0, tiled=True)  13.9 us
    mul x2, local copies, waits for them, and re-layouts, dequant(): packed.astype(jnp.float32).reshape(height, breadth // BLOCK, BLOCK)  11.4 us
  transfers between devices with their start and end apart: 3, of which 1 were waited for; matrix products, arithmetic and copies ran while one was open for 8% of the time, Pallas kernels for 0%

commit v1 on v0

v1 whole, which is shorter than its diff:
```python
import math

import jax
import jax.numpy as jnp
import numpy as np
from jax import lax
from jax.experimental import pallas as pl
from jax.experimental.pallas import tpu as pltpu
from jax.sharding import PartitionSpec as P

MESH = pl.DeviceIdType.MESH
F32 = jnp.float32
BF16 = jnp.bfloat16

EPSILON = 1e-05
ADAPTER_SCALE = 2.0
X, Y, Z = 4, 8, 8
AUDIO_ROWS, TEXT_ROWS = 32, 96
ROWS = AUDIO_ROWS + TEXT_ROWS
ENC = 1280
HALF = ENC // 2
DEC = 5120
SLAB = DEC // Y
VALUE = 1024
RANK = 64
MULTIPLIER = 1.0 / math.sqrt(X * Y * Z * 2 * ROWS)

PEERS = (1, 7, 2, 6, 3, 5, 4)


def nn(a, b):
    return lax.dot_general(a, b, (((1,), (0,)), ((), ())), preferred_element_type=F32)


def nt(a, b):
    return lax.dot_general(a, b, (((1,), (1,)), ((), ())), preferred_element_type=F32)


def tn(a, b):
    return lax.dot_general(a, b, (((0,), (0,)), ((), ())), preferred_element_type=F32)


def one_hot(rows, columns, hit):
    i = lax.broadcasted_iota(jnp.int32, (rows, columns), 0)
    j = lax.broadcasted_iota(jnp.int32, (rows, columns), 1)
    return jnp.where(hit(i, j), 1.0, 0.0).astype(BF16)


def spread(blocks):
    return one_hot(blocks, blocks * 64, lambda i, j: (j >= 64 * i) & (j < 64 * i + 64))


def erf(x):
    x = jnp.clip(x, -3.832506856900711, 3.832506856900711)
    s = x * x
    p = jnp.full_like(s, 0.00022905065861350646)
    for k in (0.0034082910107109506, 0.050955695062380861, 0.18520832239976145, 1.128379143519084):
        p = p * s + k
    q = jnp.full_like(s, -1.1791602954361697e-7)
    for k in (
        0.000023547966471313185,
        0.0010179625278914885,
        0.014070470171167667,
        0.11098505178285362,
        0.49746925110067538,
        1.0,
    ):
        q = q * s + k
    return x * p / q


def kernel(
    frames, live_frames, enc_gain, enc_q, enc_s, text, live_text, dec_gain, val_q, val_s,
    down, up, audio_cot, text_cot, source,
    out_av, out_tv, out_ag, out_tg, out_gd, out_gu,
    V, E, DT, e1, dn1, ebuf, et, et2, wv, vx, cot, xs, nrm, gn, acc, enc_f, en_p,
    R1, R2, RZs, RZr, RYs, RYr, FX,
    pair_s, pair_r, p1v_s, p1v_r, p1e_s, p1e_r, p1d_s, p1d_r,
    er_s, er_r, ed_s, ed_r, dr_s, dr_r, dd_s, dd_r, vy_s, vy_r, vx_s, vx_r, vd_s, vd_r,
    rp_s, rp_r, rz_s, rz_r, ry_s, ry_r, rx_s, rx_r,
):
    x = lax.axis_index("dp")
    f = lax.axis_index("fsdp")
    c = f % 2
    z = (f // 2) % Z
    y = f // (2 * Z)
    par = x % 2
    oc = 1 - c

    def dev(dx=0, dy=0, dz=0, core=None):
        return (
            (x + dx) % X if dx else x,
            (((y + dy) % Y if dy else y) * Z + ((z + dz) % Z if dz else z)) * 2
            + (c if core is None else core),
        )

    sibling = dev(core=oc)
    sent = []

    def send(src, dst, ss, rs, to):
        copy = pltpu.make_async_remote_copy(
            src_ref=src, dst_ref=dst, send_sem=ss, recv_sem=rs, device_id=to, device_id_type=MESH
        )
        copy.start()
        sent.append(copy)

    def got(dst, ss, rs):
        pltpu.make_async_remote_copy(
            src_ref=dst, dst_ref=dst, send_sem=ss, recv_sem=rs, device_id=sibling,
            device_id_type=MESH,
        ).wait_recv()

    barrier = pltpu.get_barrier_semaphore()
    peers = [sibling]
    peers += [dev(dx=k) for k in range(1, X)]
    peers += [dev(dy=k) for k in range(1, Y)]
    peers += [dev(dz=k) for k in range(1, Z)]
    for peer in peers:
        pl.semaphore_signal(barrier, inc=1, device_id=peer, device_id_type=MESH)

    weight = val_q[...].astype(F32) * nn(val_s[...], spread(VALUE // 64))
    for b in range(8):
        wv[b // 4, b % 4] = weight[:, 128 * b : 128 * b + 128]
    et[...] = jnp.zeros_like(et)
    et[0:10, :] = enc_q[...].astype(F32) * nn(enc_s[...], spread(ENC // 64))
    for h in range(2):
        ebuf[h] = et[:, HALF * h : HALF * (h + 1)].astype(BF16)
    dn1[z, c] = nn(down[...], one_hot(RANK, 128, lambda i, j: i == j))
    vx[c] = wv[c, pl.ds(2 * par, 2)]
    e1[y, c] = ebuf[c]

    pl.semaphore_wait(barrier, len(peers))

    send(wv.at[oc, pl.ds(2 * par, 2)], vx.at[c], pair_s.at[0], pair_r.at[0], sibling)
    send(ebuf.at[oc], e1.at[y, c], pair_s.at[1], pair_r.at[1], sibling)
    send(dn1.at[z, c], dn1.at[z, c], pair_s.at[2], pair_r.at[2], sibling)

    got(vx.at[oc], pair_s.at[0], pair_r.at[0])
    for i in range(2):
        V[c, 2 * par + i, y, pl.ds(pl.multiple_of(80 * z, 16), 80), :] = jnp.concatenate(
            [vx[0, i], vx[1, i]], axis=0
        ).astype(BF16)

    def chip_rows(zz):
        return V.at[c, pl.ds(2 * par, 2), y, pl.ds(pl.multiple_of(80 * zz, 16), 80)]

    for k in PEERS:
        send(chip_rows(z), chip_rows(z), p1v_s.at[k], p1v_r.at[k], dev(dz=k))
    got(e1.at[y, oc], pair_s.at[1], pair_r.at[1])
    for k in PEERS:
        send(e1.at[y], e1.at[y], p1e_s.at[k], p1e_r.at[k], dev(dy=k))
    got(dn1.at[z, oc], pair_s.at[2], pair_r.at[2])
    for k in PEERS:
        send(dn1.at[z], dn1.at[z], p1d_s.at[k], p1d_r.at[k], dev(dz=k))

    signal = frames[...].astype(F32)
    center = signal - jnp.mean(signal, axis=1, keepdims=True)
    variance = jnp.mean(center * center, axis=1, keepdims=True)
    en = (center * lax.rsqrt(variance + EPSILON) * enc_gain[...].astype(F32)).astype(BF16)
    feature = lax.broadcasted_iota(jnp.int32, (ENC, 128), 0)
    for b in range(ENC // 128):
        cols = slice(128 * b, 128 * b + 128)
        pick = jnp.where(feature == source[:, cols], 1.0, 0.0).astype(BF16)
        en_p[:, cols] = nn(en, pick).astype(BF16)

    for k in PEERS:
        got(e1.at[(y + 8 - k) % Y], p1e_s.at[k], p1e_r.at[k])
    for yy in range(Y):
        for cc in range(2):
            et2[20 * yy + 10 * cc : 20 * yy + 10 * cc + 10, :] = e1[yy, cc].astype(F32)[0:10]
    E[c, z] = et2[...].astype(BF16)

    def e_slab(s, d, way):
        return E.at[c, s] if d < 3 else E.at[c, s, pl.ds(80 * way, 80)]

    def e_send(d):
        send(e_slab((z + 8 - d) % Z, d, 0), e_slab((z + 8 - d) % Z, d, 0), er_s.at[0, d], er_r.at[0, d], dev(dz=1))
        send(e_slab((z + d) % Z, d, 1), e_slab((z + d) % Z, d, 1), er_s.at[1, d], er_r.at[1, d], dev(dz=7))

    def e_share(s, n):
        send(E.at[c, s], E.at[c, s], ed_s.at[n], ed_r.at[n], sibling)

    def e_step(d):
        lo, hi = (z + 7 - d) % Z, (z + 1 + d) % Z
        got(e_slab(lo, d, 0), er_s.at[0, d], er_r.at[0, d])
        got(e_slab(hi, d, 1), er_s.at[1, d], er_r.at[1, d])
        if d < 3:
            e_send(d + 1)
            e_share(lo, 1 + 2 * d)
            e_share(hi, 2 + 2 * d)
        else:
            e_share(lo, 7)

    e_send(0)
    e_share(z, 0)

    for k in PEERS:
        got(chip_rows((z + 8 - k) % Z), p1v_s.at[k], p1v_r.at[k])

    def v_blk(s, i):
        return V.at[c, 2 * par + i, s]

    def x_blk(s, i):
        return V.at[c, 2 * (1 - par) + i, s]

    def v_send(way, d, i):
        s = (y + 8 - d) % Y if way == 0 else (y + d) % Y
        send(v_blk(s, i), v_blk(s, i), vy_s.at[way, d, i], vy_r.at[way, d, i], dev(dy=1 if way == 0 else 7))

    def v_spread(s, n, i):
        send(v_blk(s, i), v_blk(s, i), vx_s.at[i, n], vx_r.at[i, n], dev(dx=1 if i == 0 else 3))
        send(v_blk(s, i), v_blk(s, i), vd_s.at[n, i], vd_r.at[n, i], sibling)

    def v_step(d, i):
        for way in range(2):
            if d == 3 and way != i:
                continue
            s = (y + 7 - d) % Y if way == 0 else (y + 1 + d) % Y
            got(v_blk(s, i), vy_s.at[way, d, i], vy_r.at[way, d, i])
            if d < 2 or (d == 2 and way == i):
                v_send(way, d + 1, i)
            v_spread(s, 7 if d == 3 else 1 + 2 * d + way, i)

    def slab_of(n):
        d = (n + 1) // 2
        return (y + 8 - d) % Y if n % 2 == 1 else (y + d) % Y

    def x_step(n):
        s = slab_of(n)
        for i in range(2):
            got(x_blk(s, i), vx_s.at[i, n], vx_r.at[i, n])
            send(x_blk(s, i), x_blk(s, i), vd_s.at[n, 2 + i], vd_r.at[n, 2 + i], sibling)

    def ready(n):
        s = slab_of(n)
        for i in range(2):
            got(V.at[oc, 2 * par + i, s], vd_s.at[n, i], vd_r.at[n, i])
            got(V.at[oc, 2 * (1 - par) + i, s], vd_s.at[n, 2 + i], vd_r.at[n, 2 + i])

    for i in range(2):
        v_send(0, 0, i)
        v_send(1, 0, i)
        v_spread(y, 0, i)

    for k in PEERS:
        got(dn1.at[(z + 8 - k) % Z], p1d_s.at[k], p1d_r.at[k])
    turned = jnp.transpose(dn1[...].reshape(SLAB, 128))
    for h in range(2):
        DT[h, y] = turned[32 * h : 32 * h + 32, :].astype(BF16)

    def d_slab(s, d, way):
        return DT.at[c, s] if d < 3 else DT.at[c, s, pl.ds(16 * way, 16)]

    def d_send(d):
        send(d_slab((y + 8 - d) % Y, d, 0), d_slab((y + 8 - d) % Y, d, 0), dr_s.at[0, d], dr_r.at[0, d], dev(dy=1))
        send(d_slab((y + d) % Y, d, 1), d_slab((y + d) % Y, d, 1), dr_s.at[1, d], dr_r.at[1, d], dev(dy=7))

    def d_step(d):
        got(d_slab((y + 7 - d) % Y, d, 0), dr_s.at[0, d], dr_r.at[0, d])
        got(d_slab((y + 1 + d) % Y, d, 1), dr_s.at[1, d], dr_r.at[1, d])
        if d < 3:
            d_send(d + 1)

    d_send(0)

    cot[0:AUDIO_ROWS, :] = audio_cot[...]
    row = lax.broadcasted_iota(jnp.int32, (TEXT_ROWS, 1), 0)
    mask = jnp.where(row < live_text[...], 1.0, 0.0)
    cot[AUDIO_ROWS:ROWS, :] = (text_cot[...].astype(F32) * mask).astype(BF16)
    bl = (ADAPTER_SCALE * nn(cot[...], up[...])).astype(BF16)
    gains = [dec_gain[:, SLAB * k : SLAB * (k + 1)].astype(F32) for k in range(Y)]
    square = jnp.zeros((TEXT_ROWS, 1), F32)
    for k in range(Y):
        part = text[:, SLAB * k : SLAB * (k + 1)].astype(F32)
        square += jnp.sum(part * part, axis=1, keepdims=True)
    inv_text = lax.rsqrt(square * (1.0 / DEC) + EPSILON)
    for k in range(Y):
        part = text[:, SLAB * k : SLAB * (k + 1)].astype(F32)
        xs[k, AUDIO_ROWS:ROWS, :] = part
        nrm[k, AUDIO_ROWS:ROWS, :] = (part * inv_text * gains[k]).astype(BF16)

    def whole(s):
        return jnp.concatenate([V[b // 4, b % 4, s] for b in range(8)], axis=1)

    def backward(n):
        s = slab_of(n)
        gn[s] = nt(cot[...], whole(s))

    def forward(n):
        s = slab_of(n)
        product = nn(nrm[s], whole(s))
        acc[...] = product if n == 0 else acc[...] + product

    e_step(0)
    d_step(0)
    v_step(0, 0)
    x_step(0)
    e_step(1)
    d_step(1)
    v_step(0, 1)
    ready(0)
    backward(0)
    v_step(1, 0)
    e_step(2)
    d_step(2)
    d_step(3)
    send(DT.at[c], DT.at[c], dd_s.at[0], dd_r.at[0], sibling)
    x_step(1)
    x_step(2)
    e_step(3)
    v_step(1, 1)

    slab_at = [z] + [(z + 7 - n // 2) % Z if n % 2 == 0 else (z + 1 + n // 2) % Z for n in range(6)] + [(z + 4) % Z]
    for n in range(8):
        got(E.at[oc, slab_at[n]], ed_s.at[n], ed_r.at[n])
    frame = lax.broadcasted_iota(jnp.int32, (4 * AUDIO_ROWS, 1), 0)
    live = jnp.where(frame < live_frames[...], 1.0, 0.0)
    for h in range(2):
        cols = slice(HALF * h, HALF * (h + 1))
        hidden = nn(en_p[...], E[h].reshape(ENC, HALF))
        gelu = 0.5 * hidden * (1.0 + erf(hidden * (1.0 / math.sqrt(2.0))))
        encoded = ((frames[:, cols].astype(F32) + gelu) * live).astype(BF16)
        for b in range(5):
            enc_f[5 * h + b] = encoded[:, 128 * b : 128 * b + 128].astype(F32)
    square = jnp.zeros((AUDIO_ROWS, 1), F32)
    for k in range(4):
        for b in range(10):
            part = enc_f[b, pl.ds(k, AUDIO_ROWS, stride=4), :]
            square += jnp.sum(part * part, axis=1, keepdims=True)
            xs[2 * k + b // 5, 0:AUDIO_ROWS, 128 * (b % 5) : 128 * (b % 5) + 128] = part
    inv_audio = lax.rsqrt(square * (1.0 / DEC) + EPSILON)
    for k in range(Y):
        nrm[k, 0:AUDIO_ROWS, :] = (xs[k, 0:AUDIO_ROWS, :] * inv_audio * gains[k]).astype(BF16)

    got(DT.at[oc], dd_s.at[0], dd_r.at[0])
    low = jnp.zeros((ROWS, RANK), F32)
    for k in range(Y):
        low += nt(nrm[k], jnp.concatenate([DT[0, k], DT[1, k]], axis=0))
    lr = low.astype(BF16)
    twice = one_hot(RANK, 128, lambda i, j: (j == i) | (j == i + RANK))
    bl2 = nn(bl, twice).astype(BF16)
    lr2 = nn(lr, twice).astype(BF16)
    first = lax.broadcasted_iota(jnp.int32, (24, 128), 1) < RANK
    g_up = tn(cot[...], lr2) * (ADAPTER_SCALE * MULTIPLIER)
    for k in range(Y):
        g_down = tn(nrm[k], bl2) * MULTIPLIER
        for zz in range(Z):
            for cc in range(2):
                at = 80 * zz + 40 * cc
                u = 16 * (Z * k + zz) + 8 * cc
                tail = jnp.concatenate([g_down[at + 24 : at + 40], g_up[u : u + 8]], axis=0)
                R1[cc, zz, 24 * k : 24 * k + 24, :] = jnp.where(first, g_down[at : at + 24], tail)
    send(R1.at[oc], R2, rp_s.at[0], rp_r.at[0], sibling)

    v_step(2, 0)
    ready(1)
    ready(2)
    backward(1)
    got(R2, rp_s.at[0], rp_r.at[0])
    for zz in range(Z):
        RZs[zz] = (R1[c, zz] + R2[zz]).astype(BF16)
    for k in PEERS:
        send(RZs.at[(z + k) % Z], RZr.at[k], rz_s.at[k], rz_r.at[k], dev(dz=k))
    v_step(2, 1)
    backward(2)
    x_step(3)
    x_step(4)
    v_step(3, 0)
    v_step(3, 1)
    forward(0)
    forward(1)
    forward(2)
    ready(3)
    ready(4)
    backward(3)
    forward(3)
    x_step(5)
    x_step(6)
    backward(4)
    forward(4)

    total = RZs[z].astype(F32)
    for k in PEERS:
        got(RZr.at[k], rz_s.at[k], rz_r.at[k])
        total += RZr[k].astype(F32)
    for yy in range(Y):
        RYs[yy] = total[24 * yy : 24 * yy + 24]
    for k in PEERS:
        send(RYs.at[(y + k) % Y], RYr.at[k], ry_s.at[k], ry_r.at[k], dev(dy=k))

    ready(5)
    ready(6)
    backward(5)
    forward(5)
    x_step(7)
    backward(6)
    forward(6)

    total = RYs[y]
    for k in PEERS:
        got(RYr.at[k], ry_s.at[k], ry_r.at[k])
        total += RYr[k]
    FX[x] = total
    for k in range(1, X):
        send(FX.at[x], FX.at[x], rx_s.at[k], rx_r.at[k], dev(dx=k))

    ready(7)
    backward(7)
    forward(7)

    values = (acc[...] + ADAPTER_SCALE * nt(lr, up[...])).astype(BF16)
    out_av[...] = values[0:AUDIO_ROWS]
    out_tv[...] = values[AUDIO_ROWS:ROWS]
    inverse = jnp.concatenate([inv_audio, inv_text], axis=0)
    mean = jnp.zeros((ROWS, 1), F32)
    for k in range(Y):
        both = jnp.concatenate([DT[0, k], DT[1, k]], axis=0)
        u = (gn[k] + nn(bl, both)) * gains[k]
        gn[k] = u
        mean += jnp.sum(u * xs[k], axis=1, keepdims=True)
    scale = inverse * inverse * inverse * (mean * (1.0 / DEC))
    for k in range(Y):
        cols = slice(SLAB * k, SLAB * (k + 1))
        grad = (inverse * gn[k] - xs[k] * scale).astype(BF16)
        out_ag[:, cols] = grad[0:AUDIO_ROWS]
        out_tg[:, cols] = grad[AUDIO_ROWS:ROWS]

    for k in range(1, X):
        got(FX.at[(x + 4 - k) % X], rx_s.at[k], rx_r.at[k])
    total = FX[0] + FX[1] + FX[2] + FX[3]
    right = pltpu.roll(total, RANK, axis=1)
    out_gd[0:24, :] = total[:, :RANK]
    out_gd[24:40, :] = right[0:16, :RANK]
    out_gu[...] = right[16:24, :RANK]

    for copy in sent:
        copy.wait_send()


def natural_features():
    place = np.arange(ENC)
    return (160 * (place % 160 // 20) + 20 * (place // 160) + place % 20).astype(np.int32)[None]


def shards(
    frames, live_frames, enc_gain, enc_q, enc_s, text, live_text, dec_gain, val_q, val_s,
    down, up, audio_cot, text_cot,
):
    dma = pltpu.SemaphoreType.DMA
    vmem = pltpu.VMEM
    return pl.pallas_call(
        kernel,
        out_shape=(
            jax.ShapeDtypeStruct((AUDIO_ROWS, VALUE), BF16),
            jax.ShapeDtypeStruct((TEXT_ROWS, VALUE), BF16),
            jax.ShapeDtypeStruct((AUDIO_ROWS, DEC), BF16),
            jax.ShapeDtypeStruct((TEXT_ROWS, DEC), BF16),
            jax.ShapeDtypeStruct((40, RANK), F32),
            jax.ShapeDtypeStruct((8, RANK), F32),
        ),
        in_specs=[pl.BlockSpec(memory_space=vmem)] * 15,
        out_specs=[pl.BlockSpec(memory_space=vmem)] * 6,
        scratch_shapes=[
            vmem((2, 4, Y, SLAB, 128), BF16),
            vmem((2, Z, 160, HALF), BF16),
            vmem((2, Y, 32, SLAB), BF16),
            vmem((Y, 2, 16, HALF), BF16),
            vmem((Z, 2, 40, 128), F32),
            vmem((2, 16, HALF), BF16),
            vmem((16, ENC), F32),
            vmem((160, HALF), F32),
            vmem((2, 4, 40, 128), F32),
            vmem((2, 2, 40, 128), F32),
            vmem((ROWS, VALUE), BF16),
            vmem((Y, ROWS, SLAB), F32),
            vmem((Y, ROWS, SLAB), BF16),
            vmem((Y, ROWS, SLAB), F32),
            vmem((ROWS, VALUE), F32),
            vmem((ENC // 128, 4 * AUDIO_ROWS, 128), F32),
            vmem((4 * AUDIO_ROWS, ENC), BF16),
            vmem((2, Z, 24 * Y, 128), F32),
            vmem((Z, 24 * Y, 128), F32),
            vmem((Z, 24 * Y, 128), BF16),
            vmem((Z, 24 * Y, 128), BF16),
            vmem((Y, 24, 128), F32),
            vmem((Y, 24, 128), F32),
            vmem((X, 24, 128), F32),
        ]
        + [
            dma(shape)
            for shape in (
                (3,), (8,), (8,), (8,), (2, 4), (8,), (2, 4), (1,), (2, 4, 2), (2, 8), (8, 4),
                (1,), (8,), (8,), (4,),
            )
            for _ in range(2)
        ],
        compiler_params=pltpu.CompilerParams(
            collective_id=0, has_side_effects=True, vmem_limit_bytes=56 * 1024 * 1024
        ),
        cost_estimate=pl.CostEstimate(
            flops=2 * ROWS * (2 * DEC * VALUE + ENC * ENC), bytes_accessed=6_000_000, transcendentals=0
        ),
    )(
        frames,
        live_frames.reshape(1, 1),
        enc_gain.reshape(1, ENC),
        enc_q,
        enc_s,
        text,
        live_text.reshape(1, 1),
        dec_gain.reshape(1, DEC),
        val_q,
        val_s,
        down,
        up,
        audio_cot,
        text_cot,
        jnp.asarray(natural_features()),
    )


def solution(mesh):
    both = ("dp", "fsdp")
    in_specs = (
        P(both, None), P(both), P(), P("fsdp", None), P("fsdp", None), P(both, None), P(both), P(),
        P("fsdp", None), P("fsdp", None), P("fsdp", None), P(), P(both, None), P(both, None),
    )
    out_specs = (
        P(both, None), P(both, None), P(both, None), P(both, None), P("fsdp", None), P("fsdp", None),
    )
    return jax.shard_map(shards, mesh=mesh, in_specs=in_specs, out_specs=out_specs, check_vma=False)
```

time: 518 us -> 97.2 us (0.19)
  the two profiles are of different devices: /device:TPU:1 before, /device:TPU:64 now
where the time goes in v1:
time: 97.2 us; the launch traced here: 96.8 us
  Pallas kernels  84 us (86%)
  local copies, waits for them, and re-layouts  10.8 us (11%)
  between operations  1.99 us (2%)
    pallas_call x1, Pallas kernels, shards(): pl.pallas_call(kernel, out_shape=(jax.ShapeDtypeStruct((AUDIO_ROWS, VALUE...  84 us
    unnamed x20, local copies, waits for them, and re-layouts  9.6 us

profile of v1, /device:TPU:64, one launch (start us, length us, event | category | flops | bytes accessed | tf_op | source)
XLA Modules:
  0.0 96.8 jit_solution(7592621320495686206)
XLA Ops:
  0.6 0.0 copy-start.4
  1.9 0.0 copy-start.3
  2.0 0.0 copy-done.4
  2.0 0.0 copy-start.2
  2.0 0.6 reshape.25.enc_gain
  2.6 0.1 copy-done.3
  2.6 0.7 copy.21.val_s
  3.3 0.0 copy-done.2
  3.3 0.6 reshape.27.dec_gain
  3.9 1.7 %copy.22.up = bf16[1024,64]{1,0:T(8,128)(2,1)} copy(bf16[1024,64]{0,1:T(8,128)(2,1)} %param.26) | data formatting | bytes 262144 | tf_op args[11]
  5.7 84.0 %shard_map.190 = (bf16[32,1024]{1,0:T(8,128)(2,1)}, bf16[96,1024]{1,0:T(8,128)(2,1)}, bf16[32,5120]{1,0:T(8,128)(2,1)}, bf16[96,5120]{1,0:T(8,128)(2,1)}, f32[40,64]{1,0:T(8,128)}, /*index=5*/f32[8,64]{1,0:T(8,128)}) custom-call(bf16[128,1280]{1,0:T(8,128)(2,1)} %frames.1, s32[1,1]{1,0:T(1,128)} %bitcast.2.live_frames, bf16[1,1280]{1,0:T(2,128)(2,1)} %reshape.25.enc_gain, ...), custom_call_target="tpu_custom_call" | custom-call | flops 3103784960 | bytes 6000000 | tf_op jit(solution)/shard_map/pallas_call | solution.py:451
  89.7 0.0 copy-start
  89.7 1.6 %copy.31 = bf16[32,1024]{1,0:T(8,128)(2,1)} copy(bf16[32,1024]{1,0:T(8,128)(2,1)} %get-tuple-element.12) | data formatting | bytes 131072
  91.3 1.6 %copy.32 = bf16[96,1024]{1,0:T(8,128)(2,1)} copy(bf16[96,1024]{1,0:T(8,128)(2,1)} %get-tuple-element.13) | data formatting | bytes 393216
  92.9 1.7 %copy.33 = bf16[32,5120]{1,0:T(8,128)(2,1)} copy(bf16[32,5120]{1,0:T(8,128)(2,1)} %get-tuple-element.14) | data formatting | bytes 655360
  94.6 0.0 copy-done
  94.6 0.0 copy-start.1
  94.6 0.9 copy.34
  95.6 0.0 copy-done.1
  95.6 0.0 copy-start.5
  95.6 0.6 copy.35
  96.2 0.1 copy-done.5
  96.2 0.6 copy.36
Async XLA Ops:
  0.6 1.3 %copy-start.4 = (bf16[1280]{0:T(1024)(128)(2,1)S(1)}, bf16[1280]{0:T(1024)(128)(2,1)}, u32[]{:S(2)}) copy-start(bf16[1280]{0:T(1024)(128)(2,1)} %param.17) | copy-start | bytes 7684
  1.9 0.7 copy-start.3
  2.0 1.4 %copy-start.2 = (bf16[5120]{0:T(1024)(128)(2,1)S(1)}, bf16[5120]{0:T(1024)(128)(2,1)}, u32[]{:S(2)}) copy-start(bf16[5120]{0:T(1024)(128)(2,1)} %param.22) | copy-start | bytes 30724
  89.7 4.9 %copy-start = (bf16[96,5120]{1,0:T(8,128)(2,1)S(1)}, bf16[96,5120]{1,0:T(8,128)(2,1)}, u32[]{:S(2)}) copy-start(bf16[96,5120]{1,0:T(8,128)(2,1)} %get-tuple-element.15) | copy-start | bytes 2949124
  94.6 0.9 copy-start.1
  95.6 0.7 copy-start.5

commit v2 on v1

--- a/solution.py
+++ b/solution.py
@@ -70,15 +70,23 @@
 
 
 def kernel(
-    frames, live_frames, enc_gain, enc_q, enc_s, text, live_text, dec_gain, val_q, val_s,
-    down, up, audio_cot, text_cot, source,
-    out_av, out_tv, out_ag, out_tg, out_gd, out_gu,
-    V, E, DT, e1, dn1, ebuf, et, et2, wv, vx, cot, xs, nrm, gn, acc, enc_f, en_p,
+    *refs,
+):
+    given, refs = refs[:15], refs[15:]
+    out_av, out_tv, out_ag, out_tg, out_gd, out_gu = refs[:6]
+    held, refs = refs[6:21], refs[21:]
+    (
+        frames, live_frames, enc_gain, enc_q, enc_s, text, live_text, dec_gain, val_q, val_s,
+        down, up, audio_cot, text_cot, source,
+    ) = held
+    (
+    V, E, DT, e1, dnp, tdn, dn1, ebuf, emine, et, et2, wv, vx, cot, xs, nrm, gn, acc, enc_f, en_p,
+    hall, hbuf,
     R1, R2, RZs, RZr, RYs, RYr, FX,
-    pair_s, pair_r, p1v_s, p1v_r, p1e_s, p1e_r, p1d_s, p1d_r,
-    er_s, er_r, ed_s, ed_r, dr_s, dr_r, dd_s, dd_r, vy_s, vy_r, vx_s, vx_r, vd_s, vd_r,
+    in_sem, pair_s, pair_r, p1v_s, p1v_r, p1e_s, p1e_r, p1d_s, p1d_r,
+    er_s, er_r, ex_s, ex_r, hp_s, hp_r, dr_s, dr_r, dd_s, dd_r, vy_s, vy_r, vx_s, vx_r, vd_s, vd_r,
     rp_s, rp_r, rz_s, rz_r, ry_s, ry_r, rx_s, rx_r,
-):
+    ) = refs
     x = lax.axis_index("dp")
     f = lax.axis_index("fsdp")
     c = f % 2
@@ -113,27 +121,48 @@
     barrier = pltpu.get_barrier_semaphore()
     peers = [sibling]
     peers += [dev(dx=k) for k in range(1, X)]
-    peers += [dev(dy=k) for k in range(1, Y)]
+    peers += [dev(dy=k, core=core) for k in range(1, Y) for core in (c, oc)]
     peers += [dev(dz=k) for k in range(1, Z)]
     for peer in peers:
         pl.semaphore_signal(barrier, inc=1, device_id=peer, device_id_type=MESH)
 
-    weight = val_q[...].astype(F32) * nn(val_s[...], spread(VALUE // 64))
+    loads = [pltpu.make_async_copy(given[i], held[i], in_sem.at[i]) for i in range(15)]
+    for i in (9, 8, 4, 3, 10, 0, 2, 14, 13, 12, 11, 6, 5, 7, 1):
+        loads[i].start()
+
+    def loaded(*indices):
+        for i in indices:
+            loads[i].wait()
+
+    def e_index(r):
+        return 2 if r == 2 else 3 * par + r
+
+    loaded(9, 8)
+    weight = val_q[...].astype(F32) * tn(val_s[...], spread(VALUE // 64))
     for b in range(8):
         wv[b // 4, b % 4] = weight[:, 128 * b : 128 * b + 128]
     et[...] = jnp.zeros_like(et)
+    loaded(4, 3)
     et[0:10, :] = enc_q[...].astype(F32) * nn(enc_s[...], spread(ENC // 64))
+    for b in range(10):
+        ebuf[b // 5, b % 5] = et[:, 128 * b : 128 * b + 128].astype(BF16)
     for h in range(2):
-        ebuf[h] = et[:, HALF * h : HALF * (h + 1)].astype(BF16)
-    dn1[z, c] = nn(down[...], one_hot(RANK, 128, lambda i, j: i == j))
+        for r in range(3):
+            emine[h, r] = ebuf[h, e_index(r)]
+    loaded(10)
+    dnp[c] = nn(down[...], one_hot(RANK, 128, lambda i, j: i == j))
+    tdn[...] = jnp.zeros_like(tdn)
     vx[c] = wv[c, pl.ds(2 * par, 2)]
-    e1[y, c] = ebuf[c]
+    e1[y, c] = emine[c]
 
     pl.semaphore_wait(barrier, len(peers))
 
     send(wv.at[oc, pl.ds(2 * par, 2)], vx.at[c], pair_s.at[0], pair_r.at[0], sibling)
-    send(ebuf.at[oc], e1.at[y, c], pair_s.at[1], pair_r.at[1], sibling)
-    send(dn1.at[z, c], dn1.at[z, c], pair_s.at[2], pair_r.at[2], sibling)
+    send(emine.at[oc], e1.at[y, c], p1e_s.at[0, 1], p1e_r.at[0, 1], sibling)
+    for k in PEERS:
+        send(emine.at[c], e1.at[y, c], p1e_s.at[k, 0], p1e_r.at[k, 0], dev(dy=k))
+        send(emine.at[oc], e1.at[y, c], p1e_s.at[k, 1], p1e_r.at[k, 1], dev(dy=k, core=oc))
+    send(dnp.at[c], dnp.at[c], pair_s.at[1], pair_r.at[1], sibling)
 
     got(vx.at[oc], pair_s.at[0], pair_r.at[0])
     for i in range(2):
@@ -146,53 +175,63 @@
 
     for k in PEERS:
         send(chip_rows(z), chip_rows(z), p1v_s.at[k], p1v_r.at[k], dev(dz=k))
-    got(e1.at[y, oc], pair_s.at[1], pair_r.at[1])
-    for k in PEERS:
-        send(e1.at[y], e1.at[y], p1e_s.at[k], p1e_r.at[k], dev(dy=k))
-    got(dn1.at[z, oc], pair_s.at[2], pair_r.at[2])
+    got(dnp.at[oc], pair_s.at[1], pair_r.at[1])
+    tdn[:, 0:80] = jnp.transpose(dnp[...].reshape(80, 128))
+    dn1[z] = tdn[pl.ds(pl.multiple_of(32 * c, 32), 32), :].astype(BF16)
     for k in PEERS:
         send(dn1.at[z], dn1.at[z], p1d_s.at[k], p1d_r.at[k], dev(dz=k))
 
+    loaded(0, 2, 14)
     signal = frames[...].astype(F32)
     center = signal - jnp.mean(signal, axis=1, keepdims=True)
     variance = jnp.mean(center * center, axis=1, keepdims=True)
-    en = (center * lax.rsqrt(variance + EPSILON) * enc_gain[...].astype(F32)).astype(BF16)
+    en = (center * lax.rsqrt(variance + EPSILON) * enc_gain[...].astype(F32).reshape(1, ENC)).astype(BF16)
     feature = lax.broadcasted_iota(jnp.int32, (ENC, 128), 0)
     for b in range(ENC // 128):
         cols = slice(128 * b, 128 * b + 128)
         pick = jnp.where(feature == source[:, cols], 1.0, 0.0).astype(BF16)
-        en_p[:, cols] = nn(en, pick).astype(BF16)
-
-    for k in PEERS:
-        got(e1.at[(y + 8 - k) % Y], p1e_s.at[k], p1e_r.at[k])
-    for yy in range(Y):
-        for cc in range(2):
-            et2[20 * yy + 10 * cc : 20 * yy + 10 * cc + 10, :] = e1[yy, cc].astype(F32)[0:10]
-    E[c, z] = et2[...].astype(BF16)
-
-    def e_slab(s, d, way):
-        return E.at[c, s] if d < 3 else E.at[c, s, pl.ds(80 * way, 80)]
-
-    def e_send(d):
-        send(e_slab((z + 8 - d) % Z, d, 0), e_slab((z + 8 - d) % Z, d, 0), er_s.at[0, d], er_r.at[0, d], dev(dz=1))
-        send(e_slab((z + d) % Z, d, 1), e_slab((z + d) % Z, d, 1), er_s.at[1, d], er_r.at[1, d], dev(dz=7))
-
-    def e_share(s, n):
-        send(E.at[c, s], E.at[c, s], ed_s.at[n], ed_r.at[n], sibling)
-
-    def e_step(d):
-        lo, hi = (z + 7 - d) % Z, (z + 1 + d) % Z
-        got(e_slab(lo, d, 0), er_s.at[0, d], er_r.at[0, d])
-        got(e_slab(hi, d, 1), er_s.at[1, d], er_r.at[1, d])
-        if d < 3:
-            e_send(d + 1)
-            e_share(lo, 1 + 2 * d)
-            e_share(hi, 2 + 2 * d)
-        else:
-            e_share(lo, 7)
-
-    e_send(0)
-    e_share(z, 0)
+        en_p[c, :, cols] = nn(en, pick).astype(BF16)
+    send(en_p.at[c], en_p.at[c], hp_s.at[0], hp_r.at[0], sibling)
+
+    got(e1.at[y, oc], p1e_s.at[0, 1], p1e_r.at[0, 1])
+    for k in PEERS:
+        got(e1.at[(y + 8 - k) % Y, c], p1e_s.at[k, 0], p1e_r.at[k, 0])
+        got(e1.at[(y + 8 - k) % Y, oc], p1e_s.at[k, 1], p1e_r.at[k, 1])
+    for r in range(3):
+        for yy in range(Y):
+            for cc in range(2):
+                et2[20 * yy + 10 * cc : 20 * yy + 10 * cc + 10, :] = e1[yy, cc, r].astype(F32)[0:10]
+        E[e_index(r), z] = et2[...].astype(BF16)
+
+    def e_part(s, d, way, r):
+        return E.at[e_index(r), s] if d < 3 else E.at[e_index(r), s, pl.ds(80 * way, 80)]
+
+    def e_send(way, d, r):
+        s = (z + 8 - d) % Z if way == 0 else (z + d) % Z
+        part = e_part(s, d, way, r)
+        send(part, part, er_s.at[way, d, r], er_r.at[way, d, r], dev(dz=1 if way == 0 else 7))
+
+    def e_across(s, n, r):
+        if r < 2:
+            send(E.at[e_index(r), s], E.at[e_index(r), s], ex_s.at[n, r], ex_r.at[n, r], dev(dx=1 if r == 0 else 3))
+
+    def e_step(d, r):
+        for way in range(2):
+            s = (z + 7 - d) % Z if way == 0 else (z + 1 + d) % Z
+            got(e_part(s, d, way, r), er_s.at[way, d, r], er_r.at[way, d, r])
+            if d < 3:
+                e_send(way, d + 1, r)
+                e_across(s, 1 + 2 * d + way, r)
+        if d == 3:
+            e_across((z + 4) % Z, 7, r)
+
+    for r in range(3):
+        e_send(0, 0, r)
+        e_send(1, 0, r)
+        e_across(z, 0, r)
+
+    e_step(0, 0)
+    e_step(0, 1)
 
     for k in PEERS:
         got(chip_rows((z + 8 - k) % Z), p1v_s.at[k], p1v_r.at[k])
@@ -208,7 +247,8 @@
         send(v_blk(s, i), v_blk(s, i), vy_s.at[way, d, i], vy_r.at[way, d, i], dev(dy=1 if way == 0 else 7))
 
     def v_spread(s, n, i):
-        send(v_blk(s, i), v_blk(s, i), vx_s.at[i, n], vx_r.at[i, n], dev(dx=1 if i == 0 else 3))
+        right = i == 0 if n in (0, 7) else i == (n + 1) % 2
+        send(v_blk(s, i), v_blk(s, i), vx_s.at[i, n], vx_r.at[i, n], dev(dx=1 if right else 3))
         send(v_blk(s, i), v_blk(s, i), vd_s.at[n, i], vd_r.at[n, i], sibling)
 
     def v_step(d, i):
@@ -225,11 +265,10 @@
         d = (n + 1) // 2
         return (y + 8 - d) % Y if n % 2 == 1 else (y + d) % Y
 
-    def x_step(n):
+    def x_step(n, i):
         s = slab_of(n)
-        for i in range(2):
-            got(x_blk(s, i), vx_s.at[i, n], vx_r.at[i, n])
-            send(x_blk(s, i), x_blk(s, i), vd_s.at[n, 2 + i], vd_r.at[n, 2 + i], sibling)
+        got(x_blk(s, i), vx_s.at[i, n], vx_r.at[i, n])
+        send(x_blk(s, i), x_blk(s, i), vd_s.at[n, 2 + i], vd_r.at[n, 2 + i], sibling)
 
     def ready(n):
         s = slab_of(n)
@@ -242,11 +281,10 @@
         v_send(1, 0, i)
         v_spread(y, 0, i)
 
+    e_step(0, 2)
     for k in PEERS:
         got(dn1.at[(z + 8 - k) % Z], p1d_s.at[k], p1d_r.at[k])
-    turned = jnp.transpose(dn1[...].reshape(SLAB, 128))
-    for h in range(2):
-        DT[h, y] = turned[32 * h : 32 * h + 32, :].astype(BF16)
+    DT[c, y] = jnp.concatenate([dn1[k].astype(F32)[:, 0:80] for k in range(Z)], axis=1).astype(BF16)
 
     def d_slab(s, d, way):
         return DT.at[c, s] if d < 3 else DT.at[c, s, pl.ds(16 * way, 16)]
@@ -263,12 +301,13 @@
 
     d_send(0)
 
+    loaded(13, 12, 11, 6, 5, 7, 1)
     cot[0:AUDIO_ROWS, :] = audio_cot[...]
     row = lax.broadcasted_iota(jnp.int32, (TEXT_ROWS, 1), 0)
     mask = jnp.where(row < live_text[...], 1.0, 0.0)
     cot[AUDIO_ROWS:ROWS, :] = (text_cot[...].astype(F32) * mask).astype(BF16)
-    bl = (ADAPTER_SCALE * nn(cot[...], up[...])).astype(BF16)
-    gains = [dec_gain[:, SLAB * k : SLAB * (k + 1)].astype(F32) for k in range(Y)]
+    bl = (ADAPTER_SCALE * nt(cot[...], up[...])).astype(BF16)
+    gains = [dec_gain[SLAB * k : SLAB * (k + 1)].astype(F32).reshape(1, SLAB) for k in range(Y)]
     square = jnp.zeros((TEXT_ROWS, 1), F32)
     for k in range(Y):
         part = text[:, SLAB * k : SLAB * (k + 1)].astype(F32)
@@ -291,33 +330,42 @@
         product = nn(nrm[s], whole(s))
         acc[...] = product if n == 0 else acc[...] + product
 
-    e_step(0)
+    e_step(1, 0)
+    e_step(1, 1)
+    e_step(1, 2)
     d_step(0)
+    e_step(2, 0)
     v_step(0, 0)
-    x_step(0)
-    e_step(1)
+    e_step(2, 1)
+    x_step(0, 0)
+    x_step(0, 1)
+    e_step(2, 2)
     d_step(1)
+    e_step(3, 0)
+    e_step(3, 1)
+    e_step(3, 2)
     v_step(0, 1)
-    ready(0)
-    backward(0)
+    d_step(2)
+
+    for n in range(8):
+        d = (n + 1) // 2
+        s = (z + 8 - d) % Z if n % 2 == 1 else (z + d) % Z
+        for r in range(2):
+            got(E.at[3 * (1 - par) + r, s], ex_s.at[n, r], ex_r.at[n, r])
+    got(en_p.at[oc], hp_s.at[0], hp_r.at[0])
+    mine = jnp.concatenate([E[b].reshape(ENC, 128) for b in range(5)], axis=1)
+    hbuf[...] = nn(en_p[...].reshape(8 * AUDIO_ROWS, ENC), mine).reshape(2, 4 * AUDIO_ROWS, HALF)
+    send(hbuf.at[oc], hall.at[c], hp_s.at[1], hp_r.at[1], sibling)
+    hall[c] = hbuf[c]
+    x_step(1, 0)
+    x_step(2, 0)
     v_step(1, 0)
-    e_step(2)
-    d_step(2)
-    d_step(3)
-    send(DT.at[c], DT.at[c], dd_s.at[0], dd_r.at[0], sibling)
-    x_step(1)
-    x_step(2)
-    e_step(3)
-    v_step(1, 1)
-
-    slab_at = [z] + [(z + 7 - n // 2) % Z if n % 2 == 0 else (z + 1 + n // 2) % Z for n in range(6)] + [(z + 4) % Z]
-    for n in range(8):
-        got(E.at[oc, slab_at[n]], ed_s.at[n], ed_r.at[n])
+    got(hall.at[oc], hp_s.at[1], hp_r.at[1])
     frame = lax.broadcasted_iota(jnp.int32, (4 * AUDIO_ROWS, 1), 0)
     live = jnp.where(frame < live_frames[...], 1.0, 0.0)
     for h in range(2):
         cols = slice(HALF * h, HALF * (h + 1))
-        hidden = nn(en_p[...], E[h].reshape(ENC, HALF))
+        hidden = hall[h]
         gelu = 0.5 * hidden * (1.0 + erf(hidden * (1.0 / math.sqrt(2.0))))
         encoded = ((frames[:, cols].astype(F32) + gelu) * live).astype(BF16)
         for b in range(5):
@@ -332,6 +380,11 @@
     for k in range(Y):
         nrm[k, 0:AUDIO_ROWS, :] = (xs[k, 0:AUDIO_ROWS, :] * inv_audio * gains[k]).astype(BF16)
 
+    d_step(3)
+    send(DT.at[c], DT.at[c], dd_s.at[0], dd_r.at[0], sibling)
+    v_step(1, 1)
+    x_step(1, 1)
+    x_step(2, 1)
     got(DT.at[oc], dd_s.at[0], dd_r.at[0])
     low = jnp.zeros((ROWS, RANK), F32)
     for k in range(Y):
@@ -352,34 +405,33 @@
                 R1[cc, zz, 24 * k : 24 * k + 24, :] = jnp.where(first, g_down[at : at + 24], tail)
     send(R1.at[oc], R2, rp_s.at[0], rp_r.at[0], sibling)
 
+    x_step(3, 0)
+    x_step(4, 0)
     v_step(2, 0)
-    ready(1)
-    ready(2)
-    backward(1)
     got(R2, rp_s.at[0], rp_r.at[0])
-    for zz in range(Z):
-        RZs[zz] = (R1[c, zz] + R2[zz]).astype(BF16)
-    for k in PEERS:
-        send(RZs.at[(z + k) % Z], RZr.at[k], rz_s.at[k], rz_r.at[k], dev(dz=k))
+    for k in PEERS:
+        at = (z + k) % Z
+        RZs[at] = (R1[c, at] + R2[at]).astype(BF16)
+        send(RZs.at[at], RZr.at[k], rz_s.at[k], rz_r.at[k], dev(dz=k))
+    for n in range(3):
+        ready(n)
+        backward(n)
+        forward(n)
     v_step(2, 1)
-    backward(2)
-    x_step(3)
-    x_step(4)
+    x_step(3, 1)
+    x_step(4, 1)
     v_step(3, 0)
     v_step(3, 1)
-    forward(0)
-    forward(1)
-    forward(2)
-    ready(3)
-    ready(4)
-    backward(3)
-    forward(3)
-    x_step(5)
-    x_step(6)
-    backward(4)
-    forward(4)
-
-    total = RZs[z].astype(F32)
+    x_step(5, 0)
+    x_step(6, 0)
+    for n in range(3, 5):
+        ready(n)
+        backward(n)
+        forward(n)
+    x_step(5, 1)
+    x_step(6, 1)
+
+    total = R1[c, z] + R2[z]
     for k in PEERS:
         got(RZr.at[k], rz_s.at[k], rz_r.at[k])
         total += RZr[k].astype(F32)
@@ -388,27 +440,16 @@
     for k in PEERS:
         send(RYs.at[(y + k) % Y], RYr.at[k], ry_s.at[k], ry_r.at[k], dev(dy=k))
 
-    ready(5)
-    ready(6)
-    backward(5)
-    forward(5)
-    x_step(7)
-    backward(6)
-    forward(6)
-
-    total = RYs[y]
-    for k in PEERS:
-        got(RYr.at[k], ry_s.at[k], ry_r.at[k])
-        total += RYr[k]
-    FX[x] = total
-    for k in range(1, X):
-        send(FX.at[x], FX.at[x], rx_s.at[k], rx_r.at[k], dev(dx=k))
-
+    for n in range(5, 7):
+        ready(n)
+        backward(n)
+        forward(n)
+    x_step(7, 0)
+    x_step(7, 1)
     ready(7)
     backward(7)
     forward(7)
-
-    values = (acc[...] + ADAPTER_SCALE * nt(lr, up[...])).astype(BF16)
+    values = (acc[...] + ADAPTER_SCALE * nn(lr, up[...])).astype(BF16)
     out_av[...] = values[0:AUDIO_ROWS]
     out_tv[...] = values[AUDIO_ROWS:ROWS]
     inverse = jnp.concatenate([inv_audio, inv_text], axis=0)
@@ -418,6 +459,15 @@
         u = (gn[k] + nn(bl, both)) * gains[k]
         gn[k] = u
         mean += jnp.sum(u * xs[k], axis=1, keepdims=True)
+
+    total = RYs[y]
+    for k in PEERS:
+        got(RYr.at[k], ry_s.at[k], ry_r.at[k])
+        total += RYr[k]
+    FX[x] = total
+    for k in range(1, X):
+        send(FX.at[x], FX.at[x], rx_s.at[k], rx_r.at[k], dev(dx=k))
+
     scale = inverse * inverse * inverse * (mean * (1.0 / DEC))
     for k in range(Y):
         cols = slice(SLAB * k, SLAB * (k + 1))
@@ -437,6 +487,20 @@
         copy.wait_send()
 
 
+def hand_over(*refs):
+    given, out, held, sems = refs[:6], refs[6:12], refs[12:18], refs[18]
+    order = (3, 2, 1, 0, 4, 5)
+    loads = [pltpu.make_async_copy(given[i], held[i], sems.at[0, i]) for i in range(6)]
+    stores = [pltpu.make_async_copy(held[i], out[i], sems.at[1, i]) for i in range(6)]
+    for i in order:
+        loads[i].start()
+    for i in order:
+        loads[i].wait()
+        stores[i].start()
+    for i in order:
+        stores[i].wait()
+
+
 def natural_features():
     place = np.arange(ENC)
     return (160 * (place % 160 // 20) + 20 * (place // 160) + place % 20).astype(np.int32)[None]
@@ -446,9 +510,26 @@
     frames, live_frames, enc_gain, enc_q, enc_s, text, live_text, dec_gain, val_q, val_s,
     down, up, audio_cot, text_cot,
 ):
+    operands = (
+        frames,
+        live_frames.reshape(1, 1),
+        enc_gain,
+        enc_q,
+        enc_s,
+        text,
+        live_text.reshape(1, 1),
+        dec_gain,
+        val_q,
+        val_s.T,
+        down,
+        up.T,
+        audio_cot,
+        text_cot,
+        jnp.asarray(natural_features()),
+    )
     dma = pltpu.SemaphoreType.DMA
     vmem = pltpu.VMEM
-    return pl.pallas_call(
+    results = pl.pallas_call(
         kernel,
         out_shape=(
             jax.ShapeDtypeStruct((AUDIO_ROWS, VALUE), BF16),
@@ -458,17 +539,21 @@
             jax.ShapeDtypeStruct((40, RANK), F32),
             jax.ShapeDtypeStruct((8, RANK), F32),
         ),
-        in_specs=[pl.BlockSpec(memory_space=vmem)] * 15,
+        in_specs=[pl.BlockSpec(memory_space=pltpu.HBM)] * 15,
         out_specs=[pl.BlockSpec(memory_space=vmem)] * 6,
         scratch_shapes=[
+            *(vmem(a.shape, a.dtype) for a in operands),
             vmem((2, 4, Y, SLAB, 128), BF16),
-            vmem((2, Z, 160, HALF), BF16),
+            vmem((5, Z, 160, 128), BF16),
             vmem((2, Y, 32, SLAB), BF16),
-            vmem((Y, 2, 16, HALF), BF16),
-            vmem((Z, 2, 40, 128), F32),
-            vmem((2, 16, HALF), BF16),
+            vmem((Y, 2, 3, 16, 128), BF16),
+            vmem((2, 40, 128), F32),
+            vmem((128, 128), F32),
+            vmem((Z, 32, 128), BF16),
+            vmem((2, 5, 16, 128), BF16),
+            vmem((2, 3, 16, 128), BF16),
             vmem((16, ENC), F32),
-            vmem((160, HALF), F32),
+            vmem((160, 128), F32),
             vmem((2, 4, 40, 128), F32),
             vmem((2, 2, 40, 128), F32),
             vmem((ROWS, VALUE), BF16),
@@ -477,7 +562,9 @@
             vmem((Y, ROWS, SLAB), F32),
             vmem((ROWS, VALUE), F32),
             vmem((ENC // 128, 4 * AUDIO_ROWS, 128), F32),
-            vmem((4 * AUDIO_ROWS, ENC), BF16),
+            vmem((2, 4 * AUDIO_ROWS, ENC), BF16),
+            vmem((2, 4 * AUDIO_ROWS, HALF), F32),
+            vmem((2, 4 * AUDIO_ROWS, HALF), F32),
             vmem((2, Z, 24 * Y, 128), F32),
             vmem((Z, 24 * Y, 128), F32),
             vmem((Z, 24 * Y, 128), BF16),
@@ -486,37 +573,30 @@
             vmem((Y, 24, 128), F32),
             vmem((X, 24, 128), F32),
         ]
+        + [dma((15,))]
         + [
             dma(shape)
             for shape in (
-                (3,), (8,), (8,), (8,), (2, 4), (8,), (2, 4), (1,), (2, 4, 2), (2, 8), (8, 4),
+                (2,), (8,), (8, 2), (8,), (2, 4, 3), (8, 2), (2,), (2, 4), (1,), (2, 4, 2), (2, 8), (8, 4),
                 (1,), (8,), (8,), (4,),
             )
             for _ in range(2)
         ],
         compiler_params=pltpu.CompilerParams(
-            collective_id=0, has_side_effects=True, vmem_limit_bytes=56 * 1024 * 1024
+            collective_id=0, has_side_effects=True, vmem_limit_bytes=60 * 1024 * 1024
         ),
         cost_estimate=pl.CostEstimate(
             flops=2 * ROWS * (2 * DEC * VALUE + ENC * ENC), bytes_accessed=6_000_000, transcendentals=0
         ),
-    )(
-        frames,
-        live_frames.reshape(1, 1),
-        enc_gain.reshape(1, ENC),
-        enc_q,
-        enc_s,
-        text,
-        live_text.reshape(1, 1),
-        dec_gain.reshape(1, DEC),
-        val_q,
-        val_s,
-        down,
-        up,
-        audio_cot,
-        text_cot,
-        jnp.asarray(natural_features()),
-    )
+    )(*operands)
+    return pl.pallas_call(
+        hand_over,
+        out_shape=tuple(jax.ShapeDtypeStruct(a.shape, a.dtype) for a in results),
+        in_specs=[pl.BlockSpec(memory_space=pl.ANY)] * 6,
+        out_specs=[pl.BlockSpec(memory_space=pl.ANY)] * 6,
+        scratch_shapes=[*(vmem(a.shape, a.dtype) for a in results), dma((2, 6))],
+        compiler_params=pltpu.CompilerParams(vmem_limit_bytes=60 * 1024 * 1024),
+    )(*results)
 
 
 def solution(mesh):

time: 97.2 us -> 85.4 us (0.88)
  the two profiles are of different devices: /device:TPU:64 before, /device:TPU:1 now
where the time goes in v2:
time: 85.4 us; the launch traced here: 85.2 us
  Pallas kernels  83.2 us (97%)
  between operations  1.94 us (2%)
    pallas_call x1, Pallas kernels, shards(): pl.pallas_call(kernel, out_shape=(jax.ShapeDtypeStruct((AUDIO_ROWS, VALUE...  80.8 us
    pallas_call x1, Pallas kernels, shards(): pl.pallas_call(hand_over, out_shape=tuple((jax.ShapeDtypeStruct(a.shape,...  2.44 us

profile of v2, /device:TPU:1, one launch (start us, length us, event | category | flops | bytes accessed | tf_op | source)
XLA Modules:
  0.0 85.2 jit_solution(9795661901976266589)
XLA Ops:
  1.9 80.8 %shard_map.190 = (bf16[32,1024]{1,0:T(8,128)(2,1)}, bf16[96,1024]{1,0:T(8,128)(2,1)}, bf16[32,5120]{1,0:T(8,128)(2,1)}, bf16[96,5120]{1,0:T(8,128)(2,1)}, f32[40,64]{1,0:T(8,128)}, /*index=5*/f32[8,64]{1,0:T(8,128)}) custom-call(bf16[128,1280]{1,0:T(8,128)(2,1)} %refs_0_.1, s32[1,1]{1,0:T(1,128)} %bitcast.4.refs_1_, bf16[1280]{0:T(1024)(128)(2,1)} %refs_2_.1, ...), custom_call_target="tpu_custom_call" | custom-call | flops 3103784960 | bytes 6000000 | tf_op jit(solution)/shard_map/pallas_call | solution.py:532
  82.7 2.4 %shard_map.191 = (bf16[32,1024]{1,0:T(8,128)(2,1)}, bf16[96,1024]{1,0:T(8,128)(2,1)}, bf16[32,5120]{1,0:T(8,128)(2,1)}, bf16[96,5120]{1,0:T(8,128)(2,1)}, f32[40,64]{1,0:T(8,128)}, /*index=5*/f32[8,64]{1,0:T(8,128)}) custom-call(bf16[32,1024]{1,0:T(8,128)(2,1)} %get-tuple-element.12.refs_0_, bf16[96,1024]{1,0:T(8,128)(2,1)} %get-tuple-element.13.refs_1_, ...), custom_call_target="tpu_custom_call" | custom-call | tf_op jit(solution)/shard_map/pallas_call | solution.py:592

commit v3 on v2

--- a/solution.py
+++ b/solution.py
@@ -26,6 +26,17 @@
 MULTIPLIER = 1.0 / math.sqrt(X * Y * Z * 2 * ROWS)
 
 PEERS = (1, 7, 2, 6, 3, 5, 4)
+
+
+ORDER = (
+    "perm", "Pe", "e00", "Pd", "Pv", "e01", "e02", "rows", "e10", "d0", "e11", "e12",
+    "v00", "e20", "e21", "e22", "d1", "e30", "e31", "e32", "v01", "d2", "x00", "x01",
+    "hid", "x10", "x20", "v10", "enc", "gd", "d3", "share", "v11", "za", "x11", "x21",
+    "gu", "v20", "zb", "x30", "x40", "b0", "f0", "v21", "x31", "x41", "b1", "f1",
+    "b2", "f2", "x50", "x60", "v30", "v31", "b3", "f3", "b4", "f4", "ya", "x51",
+    "x61", "b5", "f5", "b6", "f6", "rx", "x70", "x71", "b7", "f7", "vals", "out",
+    "fin",
+)
 
 
 def nn(a, b):
@@ -81,11 +92,11 @@
     ) = held
     (
     V, E, DT, e1, dnp, tdn, dn1, ebuf, emine, et, et2, wv, vx, cot, xs, nrm, gn, acc, enc_f, en_p,
-    hall, hbuf,
-    R1, R2, RZs, RZr, RYs, RYr, FX,
+    hall, hbuf, gain_rows,
+    RA, RA2, RAs, RAr, TA, TAr, RB, RB2, RBs, RBr, FX,
     in_sem, pair_s, pair_r, p1v_s, p1v_r, p1e_s, p1e_r, p1d_s, p1d_r,
     er_s, er_r, ex_s, ex_r, hp_s, hp_r, dr_s, dr_r, dd_s, dd_r, vy_s, vy_r, vx_s, vx_r, vd_s, vd_r,
-    rp_s, rp_r, rz_s, rz_r, ry_s, ry_r, rx_s, rx_r,
+    rp_s, rp_r, za_s, za_r, zb_s, zb_r, ya_s, ya_r, rx_s, rx_r,
     ) = refs
     x = lax.axis_index("dp")
     f = lax.axis_index("fsdp")
@@ -127,7 +138,7 @@
         pl.semaphore_signal(barrier, inc=1, device_id=peer, device_id_type=MESH)
 
     loads = [pltpu.make_async_copy(given[i], held[i], in_sem.at[i]) for i in range(15)]
-    for i in (9, 8, 4, 3, 10, 0, 2, 14, 13, 12, 11, 6, 5, 7, 1):
+    for i in (4, 3, 10, 9, 8, 0, 2, 14, 13, 12, 11, 6, 5, 7, 1):
         loads[i].start()
 
     def loaded(*indices):
@@ -137,10 +148,6 @@
     def e_index(r):
         return 2 if r == 2 else 3 * par + r
 
-    loaded(9, 8)
-    weight = val_q[...].astype(F32) * tn(val_s[...], spread(VALUE // 64))
-    for b in range(8):
-        wv[b // 4, b % 4] = weight[:, 128 * b : 128 * b + 128]
     et[...] = jnp.zeros_like(et)
     loaded(4, 3)
     et[0:10, :] = enc_q[...].astype(F32) * nn(enc_s[...], spread(ENC // 64))
@@ -149,21 +156,30 @@
     for h in range(2):
         for r in range(3):
             emine[h, r] = ebuf[h, e_index(r)]
-    loaded(10)
-    dnp[c] = nn(down[...], one_hot(RANK, 128, lambda i, j: i == j))
-    tdn[...] = jnp.zeros_like(tdn)
-    vx[c] = wv[c, pl.ds(2 * par, 2)]
     e1[y, c] = emine[c]
 
     pl.semaphore_wait(barrier, len(peers))
 
-    send(wv.at[oc, pl.ds(2 * par, 2)], vx.at[c], pair_s.at[0], pair_r.at[0], sibling)
     send(emine.at[oc], e1.at[y, c], p1e_s.at[0, 1], p1e_r.at[0, 1], sibling)
     for k in PEERS:
         send(emine.at[c], e1.at[y, c], p1e_s.at[k, 0], p1e_r.at[k, 0], dev(dy=k))
         send(emine.at[oc], e1.at[y, c], p1e_s.at[k, 1], p1e_r.at[k, 1], dev(dy=k, core=oc))
+    loaded(10)
+    dnp[c] = nn(down[...], one_hot(RANK, 128, lambda i, j: i == j))
+    tdn[...] = jnp.zeros_like(tdn)
     send(dnp.at[c], dnp.at[c], pair_s.at[1], pair_r.at[1], sibling)
-
+    loaded(9, 8)
+    weight = val_q[...].astype(F32) * tn(val_s[...], spread(VALUE // 64))
+    for b in range(8):
+        wv[b // 4, b % 4] = weight[:, 128 * b : 128 * b + 128]
+    vx[c] = wv[c, pl.ds(2 * par, 2)]
+    send(wv.at[oc, pl.ds(2 * par, 2)], vx.at[c], pair_s.at[0], pair_r.at[0], sibling)
+
+    got(dnp.at[oc], pair_s.at[1], pair_r.at[1])
+    tdn[:, 0:80] = jnp.transpose(dnp[...].reshape(80, 128))
+    dn1[z] = tdn[pl.ds(pl.multiple_of(32 * c, 32), 32), :].astype(BF16)
+    for k in PEERS:
+        send(dn1.at[z], dn1.at[z], p1d_s.at[k], p1d_r.at[k], dev(dz=k))
     got(vx.at[oc], pair_s.at[0], pair_r.at[0])
     for i in range(2):
         V[c, 2 * par + i, y, pl.ds(pl.multiple_of(80 * z, 16), 80), :] = jnp.concatenate(
@@ -175,33 +191,6 @@
 
     for k in PEERS:
         send(chip_rows(z), chip_rows(z), p1v_s.at[k], p1v_r.at[k], dev(dz=k))
-    got(dnp.at[oc], pair_s.at[1], pair_r.at[1])
-    tdn[:, 0:80] = jnp.transpose(dnp[...].reshape(80, 128))
-    dn1[z] = tdn[pl.ds(pl.multiple_of(32 * c, 32), 32), :].astype(BF16)
-    for k in PEERS:
-        send(dn1.at[z], dn1.at[z], p1d_s.at[k], p1d_r.at[k], dev(dz=k))
-
-    loaded(0, 2, 14)
-    signal = frames[...].astype(F32)
-    center = signal - jnp.mean(signal, axis=1, keepdims=True)
-    variance = jnp.mean(center * center, axis=1, keepdims=True)
-    en = (center * lax.rsqrt(variance + EPSILON) * enc_gain[...].astype(F32).reshape(1, ENC)).astype(BF16)
-    feature = lax.broadcasted_iota(jnp.int32, (ENC, 128), 0)
-    for b in range(ENC // 128):
-        cols = slice(128 * b, 128 * b + 128)
-        pick = jnp.where(feature == source[:, cols], 1.0, 0.0).astype(BF16)
-        en_p[c, :, cols] = nn(en, pick).astype(BF16)
-    send(en_p.at[c], en_p.at[c], hp_s.at[0], hp_r.at[0], sibling)
-
-    got(e1.at[y, oc], p1e_s.at[0, 1], p1e_r.at[0, 1])
-    for k in PEERS:
-        got(e1.at[(y + 8 - k) % Y, c], p1e_s.at[k, 0], p1e_r.at[k, 0])
-        got(e1.at[(y + 8 - k) % Y, oc], p1e_s.at[k, 1], p1e_r.at[k, 1])
-    for r in range(3):
-        for yy in range(Y):
-            for cc in range(2):
-                et2[20 * yy + 10 * cc : 20 * yy + 10 * cc + 10, :] = e1[yy, cc, r].astype(F32)[0:10]
-        E[e_index(r), z] = et2[...].astype(BF16)
 
     def e_part(s, d, way, r):
         return E.at[e_index(r), s] if d < 3 else E.at[e_index(r), s, pl.ds(80 * way, 80)]
@@ -225,17 +214,6 @@
         if d == 3:
             e_across((z + 4) % Z, 7, r)
 
-    for r in range(3):
-        e_send(0, 0, r)
-        e_send(1, 0, r)
-        e_across(z, 0, r)
-
-    e_step(0, 0)
-    e_step(0, 1)
-
-    for k in PEERS:
-        got(chip_rows((z + 8 - k) % Z), p1v_s.at[k], p1v_r.at[k])
-
     def v_blk(s, i):
         return V.at[c, 2 * par + i, s]
 
@@ -276,16 +254,6 @@
             got(V.at[oc, 2 * par + i, s], vd_s.at[n, i], vd_r.at[n, i])
             got(V.at[oc, 2 * (1 - par) + i, s], vd_s.at[n, 2 + i], vd_r.at[n, 2 + i])
 
-    for i in range(2):
-        v_send(0, 0, i)
-        v_send(1, 0, i)
-        v_spread(y, 0, i)
-
-    e_step(0, 2)
-    for k in PEERS:
-        got(dn1.at[(z + 8 - k) % Z], p1d_s.at[k], p1d_r.at[k])
-    DT[c, y] = jnp.concatenate([dn1[k].astype(F32)[:, 0:80] for k in range(Z)], axis=1).astype(BF16)
-
     def d_slab(s, d, way):
         return DT.at[c, s] if d < 3 else DT.at[c, s, pl.ds(16 * way, 16)]
 
@@ -299,24 +267,7 @@
         if d < 3:
             d_send(d + 1)
 
-    d_send(0)
-
-    loaded(13, 12, 11, 6, 5, 7, 1)
-    cot[0:AUDIO_ROWS, :] = audio_cot[...]
-    row = lax.broadcasted_iota(jnp.int32, (TEXT_ROWS, 1), 0)
-    mask = jnp.where(row < live_text[...], 1.0, 0.0)
-    cot[AUDIO_ROWS:ROWS, :] = (text_cot[...].astype(F32) * mask).astype(BF16)
-    bl = (ADAPTER_SCALE * nt(cot[...], up[...])).astype(BF16)
-    gains = [dec_gain[SLAB * k : SLAB * (k + 1)].astype(F32).reshape(1, SLAB) for k in range(Y)]
-    square = jnp.zeros((TEXT_ROWS, 1), F32)
-    for k in range(Y):
-        part = text[:, SLAB * k : SLAB * (k + 1)].astype(F32)
-        square += jnp.sum(part * part, axis=1, keepdims=True)
-    inv_text = lax.rsqrt(square * (1.0 / DEC) + EPSILON)
-    for k in range(Y):
-        part = text[:, SLAB * k : SLAB * (k + 1)].astype(F32)
-        xs[k, AUDIO_ROWS:ROWS, :] = part
-        nrm[k, AUDIO_ROWS:ROWS, :] = (part * inv_text * gains[k]).astype(BF16)
+    state = {}
 
     def whole(s):
         return jnp.concatenate([V[b // 4, b % 4, s] for b in range(8)], axis=1)
@@ -329,159 +280,226 @@
         s = slab_of(n)
         product = nn(nrm[s], whole(s))
         acc[...] = product if n == 0 else acc[...] + product
-
-    e_step(1, 0)
-    e_step(1, 1)
-    e_step(1, 2)
-    d_step(0)
-    e_step(2, 0)
-    v_step(0, 0)
-    e_step(2, 1)
-    x_step(0, 0)
-    x_step(0, 1)
-    e_step(2, 2)
-    d_step(1)
-    e_step(3, 0)
-    e_step(3, 1)
-    e_step(3, 2)
-    v_step(0, 1)
-    d_step(2)
-
-    for n in range(8):
-        d = (n + 1) // 2
-        s = (z + 8 - d) % Z if n % 2 == 1 else (z + d) % Z
-        for r in range(2):
-            got(E.at[3 * (1 - par) + r, s], ex_s.at[n, r], ex_r.at[n, r])
-    got(en_p.at[oc], hp_s.at[0], hp_r.at[0])
-    mine = jnp.concatenate([E[b].reshape(ENC, 128) for b in range(5)], axis=1)
-    hbuf[...] = nn(en_p[...].reshape(8 * AUDIO_ROWS, ENC), mine).reshape(2, 4 * AUDIO_ROWS, HALF)
-    send(hbuf.at[oc], hall.at[c], hp_s.at[1], hp_r.at[1], sibling)
-    hall[c] = hbuf[c]
-    x_step(1, 0)
-    x_step(2, 0)
-    v_step(1, 0)
-    got(hall.at[oc], hp_s.at[1], hp_r.at[1])
-    frame = lax.broadcasted_iota(jnp.int32, (4 * AUDIO_ROWS, 1), 0)
-    live = jnp.where(frame < live_frames[...], 1.0, 0.0)
-    for h in range(2):
-        cols = slice(HALF * h, HALF * (h + 1))
-        hidden = hall[h]
-        gelu = 0.5 * hidden * (1.0 + erf(hidden * (1.0 / math.sqrt(2.0))))
-        encoded = ((frames[:, cols].astype(F32) + gelu) * live).astype(BF16)
-        for b in range(5):
-            enc_f[5 * h + b] = encoded[:, 128 * b : 128 * b + 128].astype(F32)
-    square = jnp.zeros((AUDIO_ROWS, 1), F32)
-    for k in range(4):
-        for b in range(10):
-            part = enc_f[b, pl.ds(k, AUDIO_ROWS, stride=4), :]
+        adapter = nn(state["bl"], jnp.concatenate([DT[0, s], DT[1, s]], axis=0))
+        u = (gn[s] + adapter) * gain_rows[s]
+        gn[s] = u
+        part = jnp.sum(u * xs[s], axis=1, keepdims=True)
+        state["mean"] = part if n == 0 else state["mean"] + part
+
+
+    def twice():
+        return one_hot(RANK, 128, lambda i, j: (j == i) | (j == i + RANK))
+
+    def first(height):
+        return lax.broadcasted_iota(jnp.int32, (height, 128), 1) < RANK
+
+    def share_d():
+        send(DT.at[c], DT.at[c], dd_s.at[0], dd_r.at[0], sibling)
+
+    def do_start_e():
+        got(e1.at[y, oc], p1e_s.at[0, 1], p1e_r.at[0, 1])
+        for k in PEERS:
+            got(e1.at[(y + 8 - k) % Y, c], p1e_s.at[k, 0], p1e_r.at[k, 0])
+            got(e1.at[(y + 8 - k) % Y, oc], p1e_s.at[k, 1], p1e_r.at[k, 1])
+        for r in range(3):
+            for yy in range(Y):
+                for cc in range(2):
+                    et2[20 * yy + 10 * cc : 20 * yy + 10 * cc + 10, :] = e1[yy, cc, r].astype(F32)[0:10]
+            E[e_index(r), z] = et2[...].astype(BF16)
+
+        for r in range(3):
+            e_send(0, 0, r)
+            e_send(1, 0, r)
+            e_across(z, 0, r)
+
+    def do_start_v():
+        for k in PEERS:
+            got(chip_rows((z + 8 - k) % Z), p1v_s.at[k], p1v_r.at[k])
+
+        for i in range(2):
+            v_send(0, 0, i)
+            v_send(1, 0, i)
+            v_spread(y, 0, i)
+
+    def do_start_d():
+        for k in PEERS:
+            got(dn1.at[(z + 8 - k) % Z], p1d_s.at[k], p1d_r.at[k])
+        DT[c, y] = jnp.concatenate([dn1[k].astype(F32)[:, 0:80] for k in range(Z)], axis=1).astype(BF16)
+
+        d_send(0)
+
+    def do_perm():
+        loaded(0, 2, 14)
+        signal = frames[...].astype(F32)
+        center = signal - jnp.mean(signal, axis=1, keepdims=True)
+        variance = jnp.mean(center * center, axis=1, keepdims=True)
+        en = (center * lax.rsqrt(variance + EPSILON) * enc_gain[...].astype(F32).reshape(1, ENC)).astype(BF16)
+        feature = lax.broadcasted_iota(jnp.int32, (ENC, 128), 0)
+        for b in range(ENC // 128):
+            cols = slice(128 * b, 128 * b + 128)
+            pick = jnp.where(feature == source[:, cols], 1.0, 0.0).astype(BF16)
+            en_p[c, :, cols] = nn(en, pick).astype(BF16)
+        send(en_p.at[c], en_p.at[c], hp_s.at[0], hp_r.at[0], sibling)
+
+    def do_rows():
+        loaded(13, 12, 11, 6, 5, 7, 1)
+        cot[0:AUDIO_ROWS, :] = audio_cot[...]
+        row = lax.broadcasted_iota(jnp.int32, (TEXT_ROWS, 1), 0)
+        mask = jnp.where(row < live_text[...], 1.0, 0.0)
+        cot[AUDIO_ROWS:ROWS, :] = (text_cot[...].astype(F32) * mask).astype(BF16)
+        state["bl"] = (ADAPTER_SCALE * nt(cot[...], up[...])).astype(BF16)
+        gains = [dec_gain[SLAB * k : SLAB * (k + 1)].astype(F32).reshape(1, SLAB) for k in range(Y)]
+        for k in range(Y):
+            gain_rows[k] = gains[k]
+        square = jnp.zeros((TEXT_ROWS, 1), F32)
+        for k in range(Y):
+            part = text[:, SLAB * k : SLAB * (k + 1)].astype(F32)
             square += jnp.sum(part * part, axis=1, keepdims=True)
-            xs[2 * k + b // 5, 0:AUDIO_ROWS, 128 * (b % 5) : 128 * (b % 5) + 128] = part
-    inv_audio = lax.rsqrt(square * (1.0 / DEC) + EPSILON)
-    for k in range(Y):
-        nrm[k, 0:AUDIO_ROWS, :] = (xs[k, 0:AUDIO_ROWS, :] * inv_audio * gains[k]).astype(BF16)
-
-    d_step(3)
-    send(DT.at[c], DT.at[c], dd_s.at[0], dd_r.at[0], sibling)
-    v_step(1, 1)
-    x_step(1, 1)
-    x_step(2, 1)
-    got(DT.at[oc], dd_s.at[0], dd_r.at[0])
-    low = jnp.zeros((ROWS, RANK), F32)
-    for k in range(Y):
-        low += nt(nrm[k], jnp.concatenate([DT[0, k], DT[1, k]], axis=0))
-    lr = low.astype(BF16)
-    twice = one_hot(RANK, 128, lambda i, j: (j == i) | (j == i + RANK))
-    bl2 = nn(bl, twice).astype(BF16)
-    lr2 = nn(lr, twice).astype(BF16)
-    first = lax.broadcasted_iota(jnp.int32, (24, 128), 1) < RANK
-    g_up = tn(cot[...], lr2) * (ADAPTER_SCALE * MULTIPLIER)
-    for k in range(Y):
-        g_down = tn(nrm[k], bl2) * MULTIPLIER
-        for zz in range(Z):
-            for cc in range(2):
-                at = 80 * zz + 40 * cc
-                u = 16 * (Z * k + zz) + 8 * cc
-                tail = jnp.concatenate([g_down[at + 24 : at + 40], g_up[u : u + 8]], axis=0)
-                R1[cc, zz, 24 * k : 24 * k + 24, :] = jnp.where(first, g_down[at : at + 24], tail)
-    send(R1.at[oc], R2, rp_s.at[0], rp_r.at[0], sibling)
-
-    x_step(3, 0)
-    x_step(4, 0)
-    v_step(2, 0)
-    got(R2, rp_s.at[0], rp_r.at[0])
-    for k in PEERS:
-        at = (z + k) % Z
-        RZs[at] = (R1[c, at] + R2[at]).astype(BF16)
-        send(RZs.at[at], RZr.at[k], rz_s.at[k], rz_r.at[k], dev(dz=k))
-    for n in range(3):
+        state["inv_text"] = inv_text = lax.rsqrt(square * (1.0 / DEC) + EPSILON)
+        for k in range(Y):
+            part = text[:, SLAB * k : SLAB * (k + 1)].astype(F32)
+            xs[k, AUDIO_ROWS:ROWS, :] = part
+            nrm[k, AUDIO_ROWS:ROWS, :] = (part * inv_text * gains[k]).astype(BF16)
+
+    def do_hid():
+        for n in range(8):
+            d = (n + 1) // 2
+            s = (z + 8 - d) % Z if n % 2 == 1 else (z + d) % Z
+            for r in range(2):
+                got(E.at[3 * (1 - par) + r, s], ex_s.at[n, r], ex_r.at[n, r])
+        got(en_p.at[oc], hp_s.at[0], hp_r.at[0])
+        mine = jnp.concatenate([E[b].reshape(ENC, 128) for b in range(5)], axis=1)
+        hbuf[...] = nn(en_p[...].reshape(8 * AUDIO_ROWS, ENC), mine).reshape(2, 4 * AUDIO_ROWS, HALF)
+        send(hbuf.at[oc], hall.at[c], hp_s.at[1], hp_r.at[1], sibling)
+        hall[c] = hbuf[c]
+
+    def do_enc():
+        got(hall.at[oc], hp_s.at[1], hp_r.at[1])
+        frame = lax.broadcasted_iota(jnp.int32, (4 * AUDIO_ROWS, 1), 0)
+        live = jnp.where(frame < live_frames[...], 1.0, 0.0)
+        for h in range(2):
+            cols = slice(HALF * h, HALF * (h + 1))
+            hidden = hall[h]
+            gelu = 0.5 * hidden * (1.0 + erf(hidden * (1.0 / math.sqrt(2.0))))
+            encoded = ((frames[:, cols].astype(F32) + gelu) * live).astype(BF16)
+            for b in range(5):
+                enc_f[5 * h + b] = encoded[:, 128 * b : 128 * b + 128].astype(F32)
+        square = jnp.zeros((AUDIO_ROWS, 1), F32)
+        for k in range(4):
+            for b in range(10):
+                part = enc_f[b, pl.ds(k, AUDIO_ROWS, stride=4), :]
+                square += jnp.sum(part * part, axis=1, keepdims=True)
+                xs[2 * k + b // 5, 0:AUDIO_ROWS, 128 * (b % 5) : 128 * (b % 5) + 128] = part
+        state["inv_audio"] = inv_audio = lax.rsqrt(square * (1.0 / DEC) + EPSILON)
+        for k in range(Y):
+            nrm[k, 0:AUDIO_ROWS, :] = (xs[k, 0:AUDIO_ROWS, :] * inv_audio * gain_rows[k]).astype(BF16)
+
+    def do_gd():
+        bl2 = nn(state["bl"], twice()).astype(BF16)
+        for k in range(Y):
+            g_down = tn(nrm[k], bl2) * MULTIPLIER
+            for zz in range(Z):
+                for cc in range(2):
+                    at = 80 * zz + 40 * cc
+                    RA[cc, zz, 16 * k : 16 * k + 16, :] = jnp.where(
+                        first(16), g_down[at : at + 16], g_down[at + 24 : at + 40]
+                    )
+                    RB[cc, zz, 8 * k : 8 * k + 8, :] = g_down[at + 16 : at + 24]
+        send(RA.at[oc], RA2, rp_s.at[0], rp_r.at[0], sibling)
+
+    def do_gu():
+        got(DT.at[oc], dd_s.at[0], dd_r.at[0])
+        low = jnp.zeros((ROWS, RANK), F32)
+        for k in range(Y):
+            low += nt(nrm[k], jnp.concatenate([DT[0, k], DT[1, k]], axis=0))
+        state["lr"] = lr = low.astype(BF16)
+        lr2 = nn(lr, twice()).astype(BF16)
+        g_up = tn(cot[...], lr2) * (ADAPTER_SCALE * MULTIPLIER)
+        for k in range(Y):
+            for zz in range(Z):
+                for cc in range(2):
+                    u = 16 * (Z * k + zz) + 8 * cc
+                    part = RB[cc, zz, 8 * k : 8 * k + 8, :]
+                    RB[cc, zz, 8 * k : 8 * k + 8, :] = jnp.where(first(8), part, g_up[u : u + 8])
+        send(RB.at[oc], RB2, rp_s.at[1], rp_r.at[1], sibling)
+
+    def do_za():
+        got(RA2, rp_s.at[0], rp_r.at[0])
+        for k in PEERS:
+            at = (z + k) % Z
+            RAs[at] = (RA[c, at] + RA2[at]).astype(BF16)
+            send(RAs.at[at], RAr.at[k], za_s.at[k], za_r.at[k], dev(dz=k))
+
+    def do_zb():
+        got(RB2, rp_s.at[1], rp_r.at[1])
+        for k in PEERS:
+            at = (z + k) % Z
+            RBs[at] = (RB[c, at] + RB2[at]).astype(BF16)
+            send(RBs.at[at], RBr.at[k], zb_s.at[k], zb_r.at[k], dev(dz=k))
+
+    def do_ya():
+        part_a, part_b = RA[c, z] + RA2[z], RB[c, z] + RB2[z]
+        for k in PEERS:
+            got(RAr.at[k], za_s.at[k], za_r.at[k])
+            part_a += RAr[k].astype(F32)
+        for k in PEERS:
+            got(RBr.at[k], zb_s.at[k], zb_r.at[k])
+            part_b += RBr[k].astype(F32)
+        for yy in range(Y):
+            TA[yy, 0:16, :] = part_a[16 * yy : 16 * yy + 16]
+            TA[yy, 16:24, :] = part_b[8 * yy : 8 * yy + 8]
+        for k in PEERS:
+            send(TA.at[(y + k) % Y], TAr.at[k], ya_s.at[k], ya_r.at[k], dev(dy=k))
+
+    def do_rx():
+        total = TA[y]
+        for k in PEERS:
+            got(TAr.at[k], ya_s.at[k], ya_r.at[k])
+            total += TAr[k]
+        FX[x] = total
+        for k in range(1, X):
+            send(FX.at[x], FX.at[x], rx_s.at[k], rx_r.at[k], dev(dx=k))
+
+    def do_vals():
+        values = (acc[...] + ADAPTER_SCALE * nn(state["lr"], up[...])).astype(BF16)
+        out_av[...] = values[0:AUDIO_ROWS]
+        out_tv[...] = values[AUDIO_ROWS:ROWS]
+        inverse = jnp.concatenate([state["inv_audio"], state["inv_text"]], axis=0)
+        state["inverse"] = inverse
+
+    def do_out():
+        inverse, mean = state["inverse"], state["mean"]
+        scale = inverse * inverse * inverse * (mean * (1.0 / DEC))
+        for k in range(Y):
+            cols = slice(SLAB * k, SLAB * (k + 1))
+            grad = (inverse * gn[k] - xs[k] * scale).astype(BF16)
+            out_ag[:, cols] = grad[0:AUDIO_ROWS]
+            out_tg[:, cols] = grad[AUDIO_ROWS:ROWS]
+
+    def do_fin():
+        for k in range(1, X):
+            got(FX.at[(x + 4 - k) % X], rx_s.at[k], rx_r.at[k])
+        total = FX[0] + FX[1] + FX[2] + FX[3]
+        right = pltpu.roll(total, RANK, axis=1)
+        out_gd[0:24, :] = total[:, :RANK]
+        out_gd[24:40, :] = right[0:16, :RANK]
+        out_gu[...] = right[16:24, :RANK]
+
+    def slab(n):
         ready(n)
         backward(n)
-        forward(n)
-    v_step(2, 1)
-    x_step(3, 1)
-    x_step(4, 1)
-    v_step(3, 0)
-    v_step(3, 1)
-    x_step(5, 0)
-    x_step(6, 0)
-    for n in range(3, 5):
-        ready(n)
-        backward(n)
-        forward(n)
-    x_step(5, 1)
-    x_step(6, 1)
-
-    total = R1[c, z] + R2[z]
-    for k in PEERS:
-        got(RZr.at[k], rz_s.at[k], rz_r.at[k])
-        total += RZr[k].astype(F32)
-    for yy in range(Y):
-        RYs[yy] = total[24 * yy : 24 * yy + 24]
-    for k in PEERS:
-        send(RYs.at[(y + k) % Y], RYr.at[k], ry_s.at[k], ry_r.at[k], dev(dy=k))
-
-    for n in range(5, 7):
-        ready(n)
-        backward(n)
-        forward(n)
-    x_step(7, 0)
-    x_step(7, 1)
-    ready(7)
-    backward(7)
-    forward(7)
-    values = (acc[...] + ADAPTER_SCALE * nn(lr, up[...])).astype(BF16)
-    out_av[...] = values[0:AUDIO_ROWS]
-    out_tv[...] = values[AUDIO_ROWS:ROWS]
-    inverse = jnp.concatenate([inv_audio, inv_text], axis=0)
-    mean = jnp.zeros((ROWS, 1), F32)
-    for k in range(Y):
-        both = jnp.concatenate([DT[0, k], DT[1, k]], axis=0)
-        u = (gn[k] + nn(bl, both)) * gains[k]
-        gn[k] = u
-        mean += jnp.sum(u * xs[k], axis=1, keepdims=True)
-
-    total = RYs[y]
-    for k in PEERS:
-        got(RYr.at[k], ry_s.at[k], ry_r.at[k])
-        total += RYr[k]
-    FX[x] = total
-    for k in range(1, X):
-        send(FX.at[x], FX.at[x], rx_s.at[k], rx_r.at[k], dev(dx=k))
-
-    scale = inverse * inverse * inverse * (mean * (1.0 / DEC))
-    for k in range(Y):
-        cols = slice(SLAB * k, SLAB * (k + 1))
-        grad = (inverse * gn[k] - xs[k] * scale).astype(BF16)
-        out_ag[:, cols] = grad[0:AUDIO_ROWS]
-        out_tg[:, cols] = grad[AUDIO_ROWS:ROWS]
-
-    for k in range(1, X):
-        got(FX.at[(x + 4 - k) % X], rx_s.at[k], rx_r.at[k])
-    total = FX[0] + FX[1] + FX[2] + FX[3]
-    right = pltpu.roll(total, RANK, axis=1)
-    out_gd[0:24, :] = total[:, :RANK]
-    out_gd[24:40, :] = right[0:16, :RANK]
-    out_gu[...] = right[16:24, :RANK]
+
+    named = {
+        "Pe": do_start_e, "Pv": do_start_v, "Pd": do_start_d, "perm": do_perm, "rows": do_rows, "hid": do_hid,
+        "enc": do_enc, "gd": do_gd, "gu": do_gu, "za": do_za, "zb": do_zb, "ya": do_ya, "rx": do_rx, "vals": do_vals, "out": do_out,
+        "fin": do_fin, "share": share_d,
+    }
+    steps = {"e": e_step, "d": d_step, "v": v_step, "x": x_step, "b": slab, "f": forward}
+    for step in ORDER:
+        if step in named:
+            named[step]()
+        else:
+            steps[step[0]](*(int(digit) for digit in step[1:]))
 
     for copy in sent:
         copy.wait_send()
@@ -565,12 +583,17 @@
             vmem((2, 4 * AUDIO_ROWS, ENC), BF16),
             vmem((2, 4 * AUDIO_ROWS, HALF), F32),
             vmem((2, 4 * AUDIO_ROWS, HALF), F32),
-            vmem((2, Z, 24 * Y, 128), F32),
-            vmem((Z, 24 * Y, 128), F32),
-            vmem((Z, 24 * Y, 128), BF16),
-            vmem((Z, 24 * Y, 128), BF16),
+            vmem((Y, 1, SLAB), F32),
+            vmem((2, Z, 16 * Y, 128), F32),
+            vmem((Z, 16 * Y, 128), F32),
+            vmem((Z, 16 * Y, 128), BF16),
+            vmem((Z, 16 * Y, 128), BF16),
             vmem((Y, 24, 128), F32),
             vmem((Y, 24, 128), F32),
+            vmem((2, Z, 8 * Y, 128), F32),
+            vmem((Z, 8 * Y, 128), F32),
+            vmem((Z, 8 * Y, 128), BF16),
+            vmem((Z, 8 * Y, 128), BF16),
             vmem((X, 24, 128), F32),
         ]
         + [dma((15,))]
@@ -578,7 +601,7 @@
             dma(shape)
             for shape in (
                 (2,), (8,), (8, 2), (8,), (2, 4, 3), (8, 2), (2,), (2, 4), (1,), (2, 4, 2), (2, 8), (8, 4),
-                (1,), (8,), (8,), (4,),
+                (2,), (8,), (8,), (8,), (4,),
             )
             for _ in range(2)
         ],

time: 85.4 us -> 80.6 us (0.944)
  Pallas kernels: 83.2 us -> 78.5 us
    pallas_call x1, Pallas kernels: 80.8 us -> 76 us  [shards(): pl.pallas_call(kernel, out_shape=(jax.ShapeDtypeStruct((AUDIO_ROWS, VALUE...]
where the time goes in v3:
time: 80.6 us; the launch traced here: 80.4 us
  Pallas kernels  78.5 us (97%)
  between operations  1.94 us (2%)
    pallas_call x1, Pallas kernels, shards(): pl.pallas_call(kernel, out_shape=(jax.ShapeDtypeStruct((AUDIO_ROWS, VALUE...  76 us
    pallas_call x1, Pallas kernels, shards(): pl.pallas_call(hand_over, out_shape=tuple((jax.ShapeDtypeStruct(a.shape,...  2.44 us

profile of v3, /device:TPU:1, one launch (start us, length us, event | category | flops | bytes accessed | tf_op | source)
XLA Modules:
  0.0 80.4 jit_solution(4625156784784453442)
XLA Ops:
  1.9 76.0 %shard_map.190 = (bf16[32,1024]{1,0:T(8,128)(2,1)}, bf16[96,1024]{1,0:T(8,128)(2,1)}, bf16[32,5120]{1,0:T(8,128)(2,1)}, bf16[96,5120]{1,0:T(8,128)(2,1)}, f32[40,64]{1,0:T(8,128)}, /*index=5*/f32[8,64]{1,0:T(8,128)}) custom-call(bf16[128,1280]{1,0:T(8,128)(2,1)} %refs_0_.1, s32[1,1]{1,0:T(1,128)} %bitcast.4.refs_1_, bf16[1280]{0:T(1024)(128)(2,1)} %refs_2_.1, ...), custom_call_target="tpu_custom_call" | custom-call | flops 3103784960 | bytes 6000000 | tf_op jit(solution)/shard_map/pallas_call | solution.py:550
  78.0 2.4 %shard_map.191 = (bf16[32,1024]{1,0:T(8,128)(2,1)}, bf16[96,1024]{1,0:T(8,128)(2,1)}, bf16[32,5120]{1,0:T(8,128)(2,1)}, bf16[96,5120]{1,0:T(8,128)(2,1)}, f32[40,64]{1,0:T(8,128)}, /*index=5*/f32[8,64]{1,0:T(8,128)}) custom-call(bf16[32,1024]{1,0:T(8,128)(2,1)} %get-tuple-element.12.refs_0_, bf16[96,1024]{1,0:T(8,128)(2,1)} %get-tuple-element.13.refs_1_, ...), custom_call_target="tpu_custom_call" | custom-call | tf_op jit(solution)/shard_map/pallas_call | solution.py:615

commit v4 on v3

--- a/solution.py
+++ b/solution.py
@@ -33,8 +33,8 @@
     "v00", "e20", "e21", "e22", "d1", "e30", "e31", "e32", "v01", "d2", "x00", "x01",
     "hid", "x10", "x20", "v10", "enc", "gd", "d3", "share", "v11", "za", "x11", "x21",
     "gu", "v20", "zb", "x30", "x40", "b0", "f0", "v21", "x31", "x41", "b1", "f1",
-    "b2", "f2", "x50", "x60", "v30", "v31", "b3", "f3", "b4", "f4", "ya", "x51",
-    "x61", "b5", "f5", "b6", "f6", "rx", "x70", "x71", "b7", "f7", "vals", "out",
+    "b2", "f2", "ya", "x50", "x60", "v30", "v31", "rx", "b3", "f3", "b4", "f4",
+    "x51", "x61", "b5", "f5", "b6", "f6", "x70", "x71", "b7", "f7", "vals", "out",
     "fin",
 )
 
@@ -220,39 +220,59 @@
     def x_blk(s, i):
         return V.at[c, 2 * (1 - par) + i, s]
 
+    def v_half(q, s, j):
+        return V.at[c, q, s, pl.ds(320 * j, 320)]
+
     def v_send(way, d, i):
         s = (y + 8 - d) % Y if way == 0 else (y + d) % Y
-        send(v_blk(s, i), v_blk(s, i), vy_s.at[way, d, i], vy_r.at[way, d, i], dev(dy=1 if way == 0 else 7))
-
-    def v_spread(s, n, i):
-        right = i == 0 if n in (0, 7) else i == (n + 1) % 2
-        send(v_blk(s, i), v_blk(s, i), vx_s.at[i, n], vx_r.at[i, n], dev(dx=1 if right else 3))
-        send(v_blk(s, i), v_blk(s, i), vd_s.at[n, i], vd_r.at[n, i], sibling)
+        to = dev(dy=1 if way == 0 else 7)
+        if d < 3:
+            send(v_blk(s, i), v_blk(s, i), vy_s.at[way, d, i], vy_r.at[way, d, i], to)
+        else:
+            for j in range(2):
+                part = v_half(2 * par + i, s, j)
+                send(part, part, vy_s.at[way, d, j], vy_r.at[way, d, j], to)
+
+    def v_spread(part, n, i):
+        right = i == 0 if n in (0, 7, 8) else i == (n + 1) % 2
+        send(part, part, vx_s.at[i, n], vx_r.at[i, n], dev(dx=1 if right else 3))
+        send(part, part, vd_s.at[n, i], vd_r.at[n, i], sibling)
 
     def v_step(d, i):
         for way in range(2):
-            if d == 3 and way != i:
-                continue
             s = (y + 7 - d) % Y if way == 0 else (y + 1 + d) % Y
-            got(v_blk(s, i), vy_s.at[way, d, i], vy_r.at[way, d, i])
-            if d < 2 or (d == 2 and way == i):
-                v_send(way, d + 1, i)
-            v_spread(s, 7 if d == 3 else 1 + 2 * d + way, i)
+            if d < 3:
+                got(v_blk(s, i), vy_s.at[way, d, i], vy_r.at[way, d, i])
+                if d < 2 or way == i:
+                    v_send(way, d + 1, i)
+                v_spread(v_blk(s, i), 1 + 2 * d + way, i)
+            else:
+                part = v_half(2 * par + way, s, i)
+                got(part, vy_s.at[way, d, i], vy_r.at[way, d, i])
+                v_spread(part, 7 + i, way)
 
     def slab_of(n):
         d = (n + 1) // 2
         return (y + 8 - d) % Y if n % 2 == 1 else (y + d) % Y
 
     def x_step(n, i):
-        s = slab_of(n)
-        got(x_blk(s, i), vx_s.at[i, n], vx_r.at[i, n])
-        send(x_blk(s, i), x_blk(s, i), vd_s.at[n, 2 + i], vd_r.at[n, 2 + i], sibling)
+        if n < 7:
+            takes = ((x_blk(slab_of(n), i), n, i),)
+        else:
+            takes = tuple((v_half(2 * (1 - par) + b, slab_of(7), i), 7 + i, b) for b in range(2))
+        for part, at, b in takes:
+            got(part, vx_s.at[b, at], vx_r.at[b, at])
+            send(part, part, vd_s.at[at, 2 + b], vd_r.at[at, 2 + b], sibling)
 
     def ready(n):
         s = slab_of(n)
         for i in range(2):
-            got(V.at[oc, 2 * par + i, s], vd_s.at[n, i], vd_r.at[n, i])
-            got(V.at[oc, 2 * (1 - par) + i, s], vd_s.at[n, 2 + i], vd_r.at[n, 2 + i])
+            for q, b in ((2 * par + i, i), (2 * (1 - par) + i, 2 + i)):
+                if n < 7:
+                    got(V.at[oc, q, s], vd_s.at[n, b], vd_r.at[n, b])
+                else:
+                    for j in range(2):
+                        got(V.at[oc, q, s, pl.ds(320 * j, 320)], vd_s.at[7 + j, b], vd_r.at[7 + j, b])
 
     def d_slab(s, d, way):
         return DT.at[c, s] if d < 3 else DT.at[c, s, pl.ds(16 * way, 16)]
@@ -319,7 +339,7 @@
         for i in range(2):
             v_send(0, 0, i)
             v_send(1, 0, i)
-            v_spread(y, 0, i)
+            v_spread(v_blk(y, i), 0, i)
 
     def do_start_d():
         for k in PEERS:
@@ -600,7 +620,7 @@
         + [
             dma(shape)
             for shape in (
-                (2,), (8,), (8, 2), (8,), (2, 4, 3), (8, 2), (2,), (2, 4), (1,), (2, 4, 2), (2, 8), (8, 4),
+                (2,), (8,), (8, 2), (8,), (2, 4, 3), (8, 2), (2,), (2, 4), (1,), (2, 4, 2), (2, 9), (9, 4),
                 (2,), (8,), (8,), (8,), (4,),
             )
             for _ in range(2)

time: 80.6 us -> 84.5 us (1.048)
  Pallas kernels: 78.5 us -> 82.4 us
    pallas_call x1, Pallas kernels: 76 us -> 79.9 us  [shards(): pl.pallas_call(kernel, out_shape=(jax.ShapeDtypeStruct((AUDIO_ROWS, VALUE...]
where the time goes in v4:
time: 84.5 us; the launch traced here: 84.3 us
  Pallas kernels  82.4 us (98%)
  between operations  1.94 us (2%)
    pallas_call x1, Pallas kernels, shards(): pl.pallas_call(kernel, out_shape=(jax.ShapeDtypeStruct((AUDIO_ROWS, VALUE...  79.9 us
    pallas_call x1, Pallas kernels, shards(): pl.pallas_call(hand_over, out_shape=tuple((jax.ShapeDtypeStruct(a.shape,...  2.44 us

profile of v4, /device:TPU:1, one launch (start us, length us, event | category | flops | bytes accessed | tf_op | source)
XLA Modules:
  0.0 84.3 jit_solution(3337346520344438307)
XLA Ops:
  1.9 79.9 %shard_map.190 = (bf16[32,1024]{1,0:T(8,128)(2,1)}, bf16[96,1024]{1,0:T(8,128)(2,1)}, bf16[32,5120]{1,0:T(8,128)(2,1)}, bf16[96,5120]{1,0:T(8,128)(2,1)}, f32[40,64]{1,0:T(8,128)}, /*index=5*/f32[8,64]{1,0:T(8,128)}) custom-call(bf16[128,1280]{1,0:T(8,128)(2,1)} %refs_0_.1, s32[1,1]{1,0:T(1,128)} %bitcast.4.refs_1_, bf16[1280]{0:T(1024)(128)(2,1)} %refs_2_.1, ...), custom_call_target="tpu_custom_call" | custom-call | flops 3103784960 | bytes 6000000 | tf_op jit(solution)/shard_map/pallas_call | solution.py:570
  81.9 2.4 %shard_map.191 = (bf16[32,1024]{1,0:T(8,128)(2,1)}, bf16[96,1024]{1,0:T(8,128)(2,1)}, bf16[32,5120]{1,0:T(8,128)(2,1)}, bf16[96,5120]{1,0:T(8,128)(2,1)}, f32[40,64]{1,0:T(8,128)}, /*index=5*/f32[8,64]{1,0:T(8,128)}) custom-call(bf16[32,1024]{1,0:T(8,128)(2,1)} %get-tuple-element.12.refs_0_, bf16[96,1024]{1,0:T(8,128)(2,1)} %get-tuple-element.13.refs_1_, ...), custom_call_target="tpu_custom_call" | custom-call | tf_op jit(solution)/shard_map/pallas_call | solution.py:635
